TPU v7x, 256 devices: a whole 4x4x8 slice. The times are simulated.
256 devices in a mesh: dp: 16 (over x, z_lo), seq: 16 (over y, z_hi, core).
Axes of the slice: x: 4, y: 4, z: 8 (z_hi: 2, z_lo: 4; z = z_hi * 4 + z_lo), core: 2. Of those that a mesh axis runs over, the one named last changes fastest.
Arguments:
- dna_ids: int32 [16, 524288], P('dp', 'seq'), may hold values from 0 to 3
- stem_weight: bfloat16 [512, 768], replicated, may hold values from -0.5 to 0.5
- kernel_taps_weight: bfloat16 [3, 768, 1536], P(None, 'dp'), may hold values from -0.125 to 0.125
- query_weight: bfloat16 [1536, 512], replicated, may hold values from -3.58237875 to 3.58237875
- key_weight: bfloat16 [1536, 128], replicated, may hold values from -0.103082693 to 0.103082693
- value_weight: bfloat16 [1536, 192], replicated, may hold values from -0.15625 to 0.15625
- out_weight: bfloat16 [1536, 768], replicated, may hold values from -0.21875 to 0.21875
- cotangent: bfloat16 [16, 4096, 1536], P('dp', 'seq'), may hold values from -6 to 6
Outputs:
- layer_out: bfloat16 [16, 4096, 1536], P('dp', 'seq')
- out_weight_grad: float32 [1536, 768], P(('dp', 'seq'))
All inputs are finite; a program needn't handle non-finite values.
Results may differ from a plain program's by a relative error of at most 0.018.
Values may be sent and summed in bfloat16 or wider, within the bound.
No kernel may reach another device: no remote copies, remote signals or barrier semaphores. Data moves between devices by JAX's collectives and lax.ppermute only.
A program may use at most 128 MiB of HBM per device.

v0:
```python
import functools
import math

import jax
import jax.numpy as jnp
from jax import lax
from jax.experimental import pallas as pl
from jax.experimental.pallas import tpu as pltpu
from jax.sharding import PartitionSpec as P

HEADS = 4
HQK = 128
HV = 192
STEP = 4
NX, NY, NZ = 4, 4, 8
BF = jnp.bfloat16
F32 = jnp.float32

FIRST = ((0, 0), (3, 0), (1, 0), (2, 0), (0, 3), (0, 1), (0, 2))
SECOND = ((3, 2), (3, 3), (3, 1), (1, 2), (1, 3), (1, 1), (2, 3), (2, 1), (2, 2))


def flat(x, y, z, c):
    return (x * 4 + z % 4) * 16 + y * 4 + (z // 4) * 2 + c


def route(value, target):
    places = [(x, y, z, c) for x in range(NX) for y in range(NY) for z in range(NZ) for c in range(2)]
    pairs = [(flat(*p), flat(*target(*p))) for p in places if target(*p)]
    return lax.ppermute(value, ("dp", "seq"), pairs)


def send(value, dx=0, dy=0, dz=0, dc=0):
    return route(
        value, lambda x, y, z, c: ((x + dx) % NX, (y + dy) % NY, (z + dz) % NZ, c ^ dc)
    )


def cores(value, first, second, by):
    def target(x, y, z, c):
        to = {"x": x, "y": y, "z": z}
        axis = (first, second)[c]
        step = -by if axis == "z" and by == 2 and z % 2 else by
        to[axis] = (to[axis] + step) % {"x": NX, "y": NY, "z": NZ}[axis]
        return to["x"], to["y"], to["z"], c

    return route(value, target)


def round_ring(value, up=1):
    return route(value, lambda x, y, z, c: (x, (y + up * (1 - 2 * c)) % NY, z, c))


def dot(a, b):
    return jnp.dot(a, b, preferred_element_type=F32)


def dot_t(a, b):
    return lax.dot_general(a, b, (((1,), (1,)), ((), ())), preferred_element_type=F32)


def params():
    return pltpu.CompilerParams(vmem_limit_bytes=20 << 20)


def cost(flops, moved=1 << 20, exps=0):
    return pl.CostEstimate(flops=flops, bytes_accessed=moved, transcendentals=exps)


SMEM = pl.BlockSpec(memory_space=pltpu.SMEM)
VMEM = pl.BlockSpec(memory_space=pltpu.VMEM)


def shape(*dims, dtype=BF):
    return jax.ShapeDtypeStruct(dims, dtype)


def stem_kernel(place, sw_ref, ids_ref, far_ref, other_ref, far_other_ref, *rest):
    outs, ext = rest[:-1], rest[-1]
    refs = (ids_ref, far_ref, other_ref, far_other_ref)
    x, z_lo, y, zh, c = [place[i] for i in range(5)]
    n_rows, d0 = sw_ref.shape
    share = d0 // (len(FIRST) + len(SECOND))
    to = lax.broadcasted_iota(jnp.int32, (n_rows, n_rows), 0)
    of = lax.broadcasted_iota(jnp.int32, (n_rows, n_rows), 1)
    patch = n_rows // 4
    rows = jnp.where(of == (to % patch) * 4 + to // patch, 1.0, 0.0).astype(BF)
    sw = dot(rows, sw_ref[...]).astype(BF)
    ordered = []
    for group in (FIRST, SECOND):
        n = share * len(group)
        lane = lax.broadcasted_iota(jnp.int32, (1, n), 1)
        wanted = jnp.zeros((1, n), jnp.int32)
        for i, (near, across) in enumerate(group):
            ox, oz = jnp.where(c == 0, near, across), jnp.where(c == 0, across, near)
            start = ((x + ox) % 4 * 4 + (z_lo + oz) % 4) * share
            here = (lane >= i * share) & (lane < (i + 1) * share)
            wanted = jnp.where(here, start + lane - i * share, wanted)
        chan = lax.broadcasted_iota(jnp.int32, (d0, n), 0)
        ordered.append(dot(sw, jnp.where(chan == wanted, 1.0, 0.0).astype(BF)).astype(BF))
    n_pos = refs[0].shape[0] - 16
    edge = jnp.full((STEP, ext.shape[1]), -1.0, F32)
    first = last = edge
    for i in range(4):
        came = refs[i][n_pos:, :].astype(F32)
        first = jnp.where((y > 0) & (2 * (1 - c) + 1 - zh == i), came[16 - STEP :], first)
        last = jnp.where((y < NY - 1) & (2 * c + zh == i), came[:STEP], last)
    ext[0:8, :] = jnp.concatenate([edge, first])
    ext[8 + 4 * n_pos :, :] = jnp.concatenate([last, edge])
    blocks = [zh * 2 + c, (1 - zh) * 2 + c, zh * 2 + 1 - c, (1 - zh) * 2 + 1 - c]
    for i, b in enumerate(blocks):
        block = refs[i][:n_pos, :]
        ext[pl.ds(pl.multiple_of(8 + b * n_pos, 8), n_pos), :] = block.astype(F32)
    n = n_pos + 16
    for i, b in enumerate(blocks[2:] + blocks[:2]):
        ids = ext[pl.ds(pl.multiple_of(b * n_pos, 8), n), :]
        onehot = jnp.concatenate(
            [jnp.where(ids == k, 1.0, 0.0).astype(BF) for k in range(4)], axis=1
        )
        for g, weight in enumerate(ordered):
            stem = jax.nn.gelu(dot(onehot, weight))
            for t in range(3):
                at = STEP * (t + 1)
                outs[g * 3 + t][i * n_pos : (i + 1) * n_pos, :] = stem[at : at + n_pos].astype(BF)


def tap_weights(pieces, t):
    share = pieces[0].shape[0] // 3
    return jnp.concatenate([p[t * share : (t + 1) * share] for p in pieces])


def pack_kernel(sel, a1, a2, a3, out):
    n, half = a1.shape[0], out.shape[1]
    other = pl.ds(pl.multiple_of((1 - sel[0]) * half, half), half)
    out[:n, :] = a2[:, :half]
    out[n : 2 * n, :] = a2[:, half:]
    out[2 * n : 3 * n, :] = a1[:, other]
    out[3 * n :, :] = a3[:, other]


def pack(c, a1, a2, a3):
    rows, width = a1.shape
    return pl.pallas_call(
        pack_kernel,
        in_specs=[SMEM] + [VMEM] * 3,
        out_shape=shape(4 * rows, width // 2),
        compiler_params=params(),
        cost_estimate=cost(0),
    )(c, a1, a2, a3)


def pick_kernel(flip, sel, *refs):
    ins, out = refs[:-1], refs[-1]
    n = out.shape[0] // len(ins)
    k = 1 - sel[0] if flip else sel[0]
    for i, ref in enumerate(ins):
        out[i * n : (i + 1) * n, :] = ref[pl.ds(pl.multiple_of(k * n, 16), n), :]


def pick(c, arrays, n, flip):
    return pl.pallas_call(
        functools.partial(pick_kernel, flip),
        in_specs=[SMEM] + [VMEM] * len(arrays),
        out_shape=shape(n * len(arrays), arrays[0].shape[1]),
        compiler_params=params(),
        cost_estimate=cost(0),
    )(c, *arrays)


def conv1_kernel(sel, x0, x1, x2, own, a1, a2, a3, r, out):
    n, half = own.shape[0], out.shape[1]
    mine = pl.ds(pl.multiple_of(sel[0] * half, half), half)
    pieces = [own[:, mine], a1[:, mine], a3[:, mine], a2[:, mine]]
    pieces += [r[2 * n : 3 * n, :], r[3 * n :, :], r[pl.ds(pl.multiple_of(sel[0] * n, 16), n), :]]
    step = x0.shape[0] // 4

    def body(i, _):
        here = pl.ds(pl.multiple_of(i * step, step), step)
        total = None
        for t, x in enumerate((x0, x1, x2)):
            part = dot(x[here, :], tap_weights(pieces, t))
            total = part if total is None else total + part
        out[here, :] = total
        return 0

    lax.fori_loop(0, 4, body, 0)


def conv2_kernel(part, sel, acc, x0, x1, x2, b1, b3, swapped, last, out):
    n = last.shape[0]
    mine = pl.ds(pl.multiple_of(sel[0] * n, 16), n)
    pieces = []
    for b in (b1, b3):
        pieces += [b[mine, :], b[2 * n : 3 * n, :], b[3 * n :, :]]
    pieces += [swapped[:n, :], swapped[n:, :], last[...]]
    rows = out.shape[0] // 2
    for i in range(2):
        here = pl.ds((2 * part + i) * rows, rows)
        total = acc[here, :]
        for t, x in enumerate((x0, x1, x2)):
            total = total + dot(x[here, :], tap_weights(pieces, t))
        out[i * rows : (i + 1) * rows, :] = jax.nn.gelu(total).astype(BF)


def conv1(c, xs, pieces):
    rows, cols = xs[0].shape[0], pieces[0].shape[1] // 2
    return pl.pallas_call(
        conv1_kernel,
        in_specs=[SMEM] + [VMEM] * 8,
        out_shape=shape(rows, cols, dtype=F32),
        compiler_params=params(),
        cost_estimate=cost(6 * rows * xs[0].shape[1] * cols, 7 << 20),
    )(c, *xs, *pieces)


def conv2(c, acc, xs, pieces, part):
    rows, cols = acc.shape
    return pl.pallas_call(
        functools.partial(conv2_kernel, part),
        in_specs=[SMEM] + [VMEM] * 8,
        out_shape=shape(rows // 2, cols),
        compiler_params=params(),
        cost_estimate=cost(3 * rows * xs[0].shape[1] * cols, 4 << 20),
    )(c, acc, *xs, *pieces)


def project_kernel(sel, fk, fr, wq, wk, wv, q_mine, q_send, kv_out):
    n_pos, half, qc = fk.shape[0] // 2, fk.shape[1], wq.shape[1] // 2
    c = sel[0]
    my, other = [pl.ds(pl.multiple_of(k * half, half), half) for k in (c, 1 - c)]
    mine, theirs = [pl.ds(pl.multiple_of(k * qc, qc), qc) for k in (c, 1 - c)]
    wide_k, wide_r = fk[...].astype(F32), fr[...].astype(F32)
    squares = jnp.sum(wide_k * wide_k, -1, keepdims=True)
    squares = squares + jnp.sum(wide_r * wide_r, -1, keepdims=True)
    scale = lax.rsqrt(squares / (2 * half) + 1e-06)
    nk, nr = (wide_k * scale).astype(BF), (wide_r * scale).astype(BF)
    factor = HQK ** (-0.5) * math.log2(math.e)
    hk, hr = nk[:n_pos], nr[:n_pos]
    q_send[...] = ((dot(hk, wq[my, theirs]) + dot(hr, wq[other, theirs])) * factor).astype(BF)
    q_mine[...] = ((dot(hk, wq[my, mine]) + dot(hr, wq[other, mine])) * factor).astype(BF)
    n = 2 * n_pos
    kv_out[:n, :] = (dot(nk, wk[my, :]) + dot(nr, wk[other, :])).astype(BF)
    v = dot_t(nk, wv[:, my]) + dot_t(nr, wv[:, other])
    kv_out[n : 2 * n, :] = v[:, :128].astype(BF)
    tail = v[:, 128:]
    kv_out[2 * n :, :] = jnp.concatenate([tail[:n_pos], tail[n_pos:]], axis=1).astype(BF)


def project(c, f_keep, f_recv, query_weight, key_weight, value_weight):
    n, half = f_keep.shape
    n_pos = n // 2
    qc = query_weight.shape[1] // 2
    return pl.pallas_call(
        project_kernel,
        in_specs=[SMEM] + [VMEM] * 5,
        out_shape=[shape(n_pos, qc), shape(n_pos, qc), shape(5 * n_pos, 128)],
        compiler_params=params(),
        cost_estimate=cost(4 * n * half * 640, 4 << 20),
    )(c, f_keep, f_recv, query_weight, key_weight, value_weight)


def unpack(packed):
    n = packed.shape[0] // 5
    k, va, tail = packed[: 2 * n], packed[2 * n : 4 * n], packed[4 * n :]
    tail = tail.astype(F32)
    tail = jnp.concatenate([tail, pltpu.roll(tail, 64, 1)])
    lane = lax.broadcasted_iota(jnp.int32, tail.shape, 1)
    tail = jnp.where(lane < HV - 128, tail, jnp.where(lane == HV - 128, 1.0, 0.0))
    return k, jnp.concatenate([va, tail.astype(BF)], axis=1)


def attend_kernel(groups, first, last, *refs):
    qs = refs[:2]
    at = 2
    kvs = []
    for n in groups:
        kvs.append(unpack(jnp.concatenate([r[...] for r in refs[at : at + n]])))
        at += n
    rest = refs[at:]
    if not first:
        m_in, acc_in = rest[:2]
        rest = rest[2:]
    rows = qs[0].shape[0]
    for w in range(2):
        for h in range(HEADS // 2):
            q = qs[w][:, h * HQK : (h + 1) * HQK]
            scores = [dot_t(q, k) for k, _ in kvs]
            top = functools.reduce(
                jnp.maximum, [jnp.max(s, axis=1, keepdims=True) for s in scores]
            )
            here = pl.ds((w * 2 + h) * rows, rows)
            if not first:
                before = m_in[here, :1]
                top = jnp.maximum(top, before)
            total = None
            for s, (_, v) in zip(scores, kvs):
                part = dot(jnp.exp2(s - top).astype(BF), v)
                total = part if total is None else total + part
            if not first:
                total = total + acc_in[here, :] * jnp.exp2(before - top)
            if last:
                norm = total[:, :HV] / total[:, HV : HV + 1]
                rest[0][w * rows : (w + 1) * rows, h * HV : (h + 1) * HV] = norm.astype(BF)
            else:
                rest[0][here, :] = jnp.broadcast_to(top, (rows, 128))
                rest[1][here, :] = total


def attend(qs, kvs, state, last):
    rows = qs[0].shape[0]
    if last:
        out = shape(2 * rows, HEADS // 2 * HV)
    else:
        out = (shape(4 * rows, 128, dtype=F32), shape(4 * rows, 256, dtype=F32))
    n = sum(kv.shape[0] for group in kvs for kv in group) * 2 // 5
    return pl.pallas_call(
        functools.partial(attend_kernel, tuple(len(g) for g in kvs), not state, last),
        out_shape=out,
        compiler_params=params(),
        cost_estimate=cost(0),
    )(*qs, *[kv for group in kvs for kv in group], *state)


def finish_kernel(sel, fk, fr, attn, theirs, w, out):
    n_pos, cols = theirs.shape
    half = fk.shape[1]
    c = sel[0]
    mine, other = [pl.ds(pl.multiple_of(k * cols, cols), cols) for k in (c, 1 - c)]
    a, b = attn[:n_pos, :], theirs[...]
    ours, far = fk[:n_pos, :].astype(F32), fr[:n_pos, :].astype(F32)
    for k in range(2):
        rows = slice(k * half, (k + 1) * half)
        total = jnp.where(c == k, ours, far) + dot_t(a, w[rows, mine]) + dot_t(b, w[rows, other])
        out[:, rows] = total.astype(BF)


def finish(c, f_keep, f_recv, attn, theirs, out_weight):
    n_pos, cols = theirs.shape
    width = out_weight.shape[0]
    return pl.pallas_call(
        finish_kernel,
        in_specs=[SMEM] + [VMEM] * 5,
        out_shape=shape(n_pos, width),
        compiler_params=params(),
        cost_estimate=cost(4 * n_pos * width * cols, 4 << 20),
    )(c, f_keep, f_recv, attn, theirs, out_weight)


def grad_kernel(at, cot, cot_far, attn, own, one, two, three, total):
    n_pos, block = cot.shape[0], cot.shape[1] // 4
    a, b = attn[:n_pos, :], attn[n_pos:, :]
    down = lambda u, v: lax.dot_general(u, v, (((0,), (0,)), ((), ())), preferred_element_type=F32)
    for k in range(4):
        here = slice(k * block, (k + 1) * block)
        total[here, :] = down(cot[:, here], a) + down(cot_far[:, here], b)
    n = block // 16
    for k, out in enumerate((own, one, two, three)):
        x, y = (at[0] + k) % 4, (at[1] + k) % 4
        for i in range(16):
            start = jnp.where(at[2] == 0, x * block + i * n, i * 4 * n + y * n)
            rows = pl.ds(pl.multiple_of(start, 8), n)
            out[i * n : (i + 1) * n, :] = total[rows, :].astype(out.dtype)


def quarters(rows, cols):
    return [shape(rows, cols, dtype=F32)] + [shape(rows, cols)] * 3


def gradient(at, cot, cot_far, attn):
    block, cols = cot.shape[1] // 4, attn.shape[1]
    return pl.pallas_call(
        grad_kernel,
        in_specs=[SMEM] + [VMEM] * 3,
        out_shape=quarters(block, cols),
        scratch_shapes=[pltpu.VMEM((cot.shape[1], cols), F32)],
        compiler_params=params(),
        cost_estimate=cost(16 * cot.shape[0] * block * cols, 3 << 20),
    )(at, cot, cot_far, attn)


def chunks_kernel(at, own, a, b, d, out, total):
    total[...] = own[...] + a[...].astype(F32) + b[...].astype(F32) + d[...].astype(F32)
    n = out.shape[1]
    for j in range(4):
        for zl in range(4):
            start = jnp.where(at[2] == 0, zl * 4 + j, j * 4 + zl) * 2 * n
            rows = total[pl.ds(pl.multiple_of(start, 8), 2 * n), :].astype(BF)
            out[j * 8 + zl] = rows[:n]
            out[j * 8 + 4 + zl] = rows[n:]


def chunks_of(at, own, came):
    rows, cols = own.shape
    return pl.pallas_call(
        chunks_kernel,
        in_specs=[SMEM] + [VMEM] * 4,
        out_shape=shape(32, rows // 32, cols),
        scratch_shapes=[pltpu.VMEM((rows, cols), F32)],
        compiler_params=params(),
        cost_estimate=cost(rows * cols * 4),
    )(at, own, *came)


def gather_kernel(sel, came, keep, away):
    total = jnp.sum(came[...].astype(F32), axis=0)
    n = total.shape[0] // 2
    keep[...] = jnp.where(sel[0] == 0, total[:n], total[n:])
    away[...] = jnp.where(sel[0] == 0, total[n:], total[:n])


def gathered(c, came):
    _, rows, cols = came.shape
    return pl.pallas_call(
        gather_kernel,
        in_specs=[SMEM, VMEM],
        out_shape=[shape(rows // 2, cols, dtype=F32)] * 2,
        compiler_params=params(),
        cost_estimate=cost(rows * cols * 32),
    )(c, came)


def join_kernel(sel, keep, away, out):
    cols = keep.shape[1]
    out[:, :cols] = jnp.where(sel[0] == 0, keep[...], away[...])
    out[:, cols:] = jnp.where(sel[0] == 0, away[...], keep[...])


def join(c, keep, away):
    rows, cols = keep.shape
    return pl.pallas_call(
        join_kernel,
        in_specs=[SMEM] + [VMEM] * 2,
        out_shape=shape(rows, 2 * cols, dtype=F32),
        compiler_params=params(),
        cost_estimate=cost(0),
    )(c, keep, away)


def local(
    dna_ids,
    stem_weight,
    kernel_taps_weight,
    query_weight,
    key_weight,
    value_weight,
    out_weight,
    cotangent,
):
    patch = stem_weight.shape[0] // 4
    n_pos = dna_ids.shape[1] // patch
    share, width = kernel_taps_weight.shape[1:]
    dp, seq = lax.axis_index("dp"), lax.axis_index("seq")
    x, zl = dp // 4, dp % 4
    y, zh, c = seq // 4, (seq // 2) % 2, seq % 2
    core = c.astype(jnp.int32).reshape(1)
    place = jnp.stack([x, zl, y, zh, c]).astype(jnp.int32)
    at = jnp.stack([x, y, c]).astype(jnp.int32)
    core, place, at, dna_ids = lax.optimization_barrier((core, place, at, dna_ids))
    cat = lambda *a: jnp.concatenate(a)

    own = kernel_taps_weight.reshape(3 * share, width)
    a1, a3, a2 = [cores(own, "x", "z", k) for k in (1, -1, 2)]

    ids = lax.optimization_barrier(dna_ids.reshape(n_pos, patch).astype(BF))
    end = jnp.where(c == 1, ids[-16:], ids[:16])
    ids = cat(ids, round_ring(end, -1))
    far, other = send(ids, dz=4), send(ids, dc=1)

    widths = [share * len(g) for g in (FIRST, SECOND)]
    far, other, a1, a2, a3 = lax.optimization_barrier((far, other, a1, a2, a3))
    far_other = send(far, dc=1)
    xs = pl.pallas_call(
        stem_kernel,
        in_specs=[SMEM] + [VMEM] * 5,
        out_shape=[shape(4 * n_pos, n) for n in widths for _ in range(3)],
        scratch_shapes=[pltpu.VMEM((4 * n_pos + 16, patch), F32)],
        compiler_params=params(),
        cost_estimate=cost(4 * 10**9, 8 << 20),
    )(place, stem_weight, ids, far, other, far_other)

    r = send(pack(core, a1, a2, a3), dc=1)
    b1, b3 = cores(r, "x", "z", 1), cores(r, "x", "z", -1)
    last = cores(pick(core, [r], 3 * share, False), "x", "z", 2)
    cot = cotangent[0]
    cot_far = send(cot, dc=1)

    acc = conv1(core, xs[:3], [own, a1, a2, a3, r])
    b1, b3, last, acc = lax.optimization_barrier((b1, b3, last, acc))
    pieces = [b1, b3, send(pick(core, [b1, b3], 3 * share, True), dc=1), last]
    f_recv = send(conv2(core, acc, xs[3:], pieces, 0), dc=1)
    f_keep = conv2(core, acc, xs[3:], pieces, 1)
    q_mine, q_send, kv = project(core, f_keep, f_recv, query_weight, key_weight, value_weight.T)

    r1, r2 = round_ring(kv), round_ring(kv, -1)
    qs = [q_mine, send(q_send, dc=1)]
    state = attend(qs, [[kv], [send(kv, dc=1)]], (), False)
    r1, r2, *state = lax.optimization_barrier((r1, r2, *state))
    rr = round_ring(r1)
    r1_o, r2_o = send(r1, dc=1), send(r2, dc=1)
    state = attend(qs, [[r1], [r2]], state, False)
    state = attend(qs, [[r1_o], [r2_o]], state, False)
    rr, *state = lax.optimization_barrier((rr, *state))
    attn = attend(qs, [[rr], [send(rr, dc=1)]], state, True)

    own_part, *parts = gradient(at, cot, cot_far, attn)
    came = [cores(parts[k - 1], "x", "y", k) for k in (2, 1, 3)]
    attn, *_ = lax.optimization_barrier((attn, parts[0]))
    theirs = send(attn[n_pos:], dc=1)
    layer_out = finish(core, f_keep, f_recv, attn, theirs, out_weight)
    layer_out, *came = lax.optimization_barrier((layer_out, *came))
    chunks = chunks_of(at, own_part, came)
    groups = [[flat(i, j, k, 0) for j in range(NY) for k in range(NZ)] for i in range(NX)]
    groups += [[flat(i, j, k, 1) for i in range(NX) for k in range(NZ)] for j in range(NY)]
    came = lax.all_to_all(chunks, ("dp", "seq"), 0, 0, axis_index_groups=groups)
    keep, away = gathered(core, came)
    away = send(away, dc=1)
    out_grad = join(core, keep, away)
    return (layer_out[None], out_grad)


def solution(mesh):
    placed = (P("dp", "seq"), P(), P(None, "dp", None), P(), P(), P(), P(), P("dp", "seq", None))
    return jax.shard_map(
        local,
        mesh=mesh,
        in_specs=placed,
        out_specs=(P("dp", "seq", None), P(("dp", "seq"), None)),
        check_vma=False,
    )
```

profile of v0, /device:TPU:1, one launch (start us, length us, event | category | flops | bytes accessed | tf_op | source)
XLA Modules:
  0.0 113.3 jit_solution(5845475934992793035)
XLA Ops:
  0.6 2.5 %collective-permute-start.3 = (bf16[144,1536]{1,0:T(8,128)(2,1)}, bf16[144,1536]{1,0:T(8,128)(2,1)S(1)}, u32[]{:S(2)}, u32[]{:S(2)}) collective-permute-start(bf16[144,1536]{1,0:T(8,128)(2,1)} %bitcast.11), channel_id=1, source_target_pairs={{0,64},{1,17},{16,80},{17,33},{32,96},{33,49},{48,112},{49,3},{2,6... | collective-permute-start | bytes 1327112 | tf_op jit(solution)/shard_map/ppermute | solution.py:30
  3.2 3.0 %collective-permute-start.4 = (bf16[144,1536]{1,0:T(8,128)(2,1)}, bf16[144,1536]{1,0:T(8,128)(2,1)S(1)}, u32[]{:S(2)}, u32[]{:S(2)}) collective-permute-start(bf16[144,1536]{1,0:T(8,128)(2,1)} %bitcast.12), channel_id=1, source_target_pairs={{0,128},{1,33},{16,144},{17,51},{32,160},{33,3},{48,176},{49,17},{... | collective-permute-start | bytes 1327112 | tf_op jit(solution)/shard_map/ppermute | solution.py:30
  6.2 2.9 %collective-permute-start.5 = (bf16[144,1536]{1,0:T(8,128)(2,1)}, bf16[144,1536]{1,0:T(8,128)(2,1)S(1)}, u32[]{:S(2)}, u32[]{:S(2)}) collective-permute-start(bf16[144,1536]{1,0:T(8,128)(2,1)} %bitcast.13), channel_id=1, source_target_pairs={{0,192},{1,51},{16,208},{17,1},{32,224},{33,17},{48,240},{49,33},{... | collective-permute-start | bytes 1327112 | tf_op jit(solution)/shard_map/ppermute | solution.py:30
  10.5 1.4 %collective-permute-start = (bf16[16,128]{1,0:T(8,128)(2,1)S(1)}, bf16[16,128]{1,0:T(8,128)(2,1)S(1)}, u32[]{:S(2)}, u32[]{:S(2)}) collective-permute-start(bf16[16,128]{1,0:T(8,128)(2,1)S(1)} %slice_select_fusion), channel_id=1, source_target_pairs={{0,12},{1,5},{16,28},{17,21},{32,44},{33,37},{48,60},{49,53},{2,14... | collective-permute-start | bytes 12296 | tf_op jit(solution)/shard_map/ppermute | solution.py:30
  11.9 2.7 %collective-permute-done = bf16[16,128]{1,0:T(8,128)(2,1)S(1)} collective-permute-done((bf16[16,128]{1,0:T(8,128)(2,1)S(1)}, bf16[16,128]{1,0:T(8,128)(2,1)S(1)}, u32[]{:S(2)}, u32[]{:S(2)}) %collective-permute-start) | collective-permute-done | bytes 4128 | tf_op jit(solution)/shard_map/ppermute | solution.py:30
  14.6 2.1 %collective-permute-start.1 = (bf16[272,128]{1,0:T(8,128)(2,1)S(1)}, bf16[272,128]{1,0:T(8,128)(2,1)S(1)}, u32[]{:S(2)}, u32[]{:S(2)}) collective-permute-start(bf16[272,128]{1,0:T(8,128)(2,1)S(1)} %pad_maximum_fusion.ids_ref), channel_id=1, source_target_pairs={{0,2},{1,3},{16,18},{17,19},{32,34},{33,35},{48,50},{49,51},{2,0},... | collective-permute-start | bytes 208904 | tf_op jit(solution)/shard_map/ppermute | solution.py:30
  16.7 4.2 %collective-permute-start.2 = (bf16[272,128]{1,0:T(8,128)(2,1)S(1)}, bf16[272,128]{1,0:T(8,128)(2,1)S(1)}, u32[]{:S(2)}, u32[]{:S(2)}) collective-permute-start(bf16[272,128]{1,0:T(8,128)(2,1)S(1)} %pad_maximum_fusion.ids_ref), channel_id=1, source_target_pairs={{0,1},{1,0},{16,17},{17,16},{32,33},{33,32},{48,49},{49,48},{2,3},... | collective-permute-start | bytes 208904 | tf_op jit(solution)/shard_map/ppermute | solution.py:30
  21.9 1.7 %collective-permute-start.6 = (bf16[576,768]{1,0:T(8,128)(2,1)S(1)}, bf16[576,768]{1,0:T(8,128)(2,1)S(1)}, u32[]{:S(2)}, u32[]{:S(2)}) collective-permute-start(bf16[576,768]{1,0:T(8,128)(2,1)S(1)} %shard_map.95), channel_id=1, source_target_pairs={{0,1},{1,0},{16,17},{17,16},{32,33},{33,32},{48,49},{49,48},{2,3},... | collective-permute-start | bytes 2654216 | tf_op jit(solution)/shard_map/ppermute | solution.py:30
  23.6 2.1 %collective-permute-done.6.refs_0_.r = bf16[576,768]{1,0:T(8,128)(2,1)S(1)} collective-permute-done((bf16[576,768]{1,0:T(8,128)(2,1)S(1)}, bf16[576,768]{1,0:T(8,128)(2,1)S(1)}, u32[]{:S(2)}, u32[]{:S(2)}) %collective-permute-start.6) | collective-permute-done | bytes 884768 | tf_op jit(solution)/shard_map/ppermute | solution.py:30
  25.7 2.9 %collective-permute-start.7 = (bf16[576,768]{1,0:T(8,128)(2,1)S(1)}, bf16[576,768]{1,0:T(8,128)(2,1)S(1)}, u32[]{:S(2)}, u32[]{:S(2)}) collective-permute-start(bf16[576,768]{1,0:T(8,128)(2,1)S(1)} %collective-permute-done.6.refs_0_.r), channel_id=1, source_target_pairs={{0,64},{1,17},{16,80},{17,33},{32,96},{33,49},{48,112},{49,3},{2,6... | collective-permute-start | bytes 2654216 | tf_op jit(solution)/shard_map/ppermute | solution.py:30
  28.6 2.1 %collective-permute-start.8 = (bf16[576,768]{1,0:T(8,128)(2,1)S(1)}, bf16[576,768]{1,0:T(8,128)(2,1)S(1)}, u32[]{:S(2)}, u32[]{:S(2)}) collective-permute-start(bf16[576,768]{1,0:T(8,128)(2,1)S(1)} %collective-permute-done.6.refs_0_.r), channel_id=1, source_target_pairs={{0,192},{1,51},{16,208},{17,1},{32,224},{33,17},{48,240},{49,33},{... | collective-permute-start | bytes 2654216 | tf_op jit(solution)/shard_map/ppermute | solution.py:30
  32.0 3.8 %shard_map.97 = (bf16[1024,336]{1,0:T(8,128)(2,1)S(1)}, bf16[1024,336]{1,0:T(8,128)(2,1)S(1)}, bf16[1024,336]{1,0:T(8,128)(2,1)S(1)}, bf16[1024,432]{1,0:T(8,128...) custom-call(s32[5]{0:T(128)S(1)} %stack.26.place, bf16[512,768]{1,0:T(8,128)(2,1)S(1)} %copy-done.5, ...), custom_call_target="tpu_custom_call" | custom-call | flops 4000000000 | bytes 8388608 | tf_op jit(solution)/shard_map/pallas_call | solution.py:472
  35.8 3.2 %shard_map.98.acc = f32[1024,768]{1,0:T(8,128)S(1)} custom-call(s32[1]{0:T(128)} %bitcast.sel, bf16[1024,336]{1,0:T(8,128)(2,1)S(1)} %get-tuple-element.56.x0, bf16[1024,336]{1,0:T(8,128)(2,1)S(1)} %get-tuple-element.57.x1, bf16[1024,336]{1,0:T(8,128)(2,1)S(1)} %get-tuple-element.58.x2, bf16[144,1536]{1,0:T(8,128)(2,1)S(1)} %bitcast.14, ...), custom_call_target="tpu_custom_call" | custom-call | flops 1585446912 | bytes 7340032 | tf_op jit(solution)/shard_map/pallas_call | solution.py:207
  39.0 5.7 %collective-permute-done.9.last = bf16[144,768]{1,0:T(8,128)(2,1)S(1)} collective-permute-done((bf16[144,768]{1,0:T(8,128)(2,1)S(1)}, bf16[144,768]{1,0:T(8,128)(2,1)S(1)}, u32[]{:S(2)}, u32[]{:S(2)}) %collective-permute-start.9) | collective-permute-done | bytes 221216 | tf_op jit(solution)/shard_map/ppermute | solution.py:30
  45.0 1.8 %collective-permute-done.11.swapped = bf16[288,768]{1,0:T(8,128)(2,1)S(1)} collective-permute-done((bf16[288,768]{1,0:T(8,128)(2,1)S(1)}, bf16[288,768]{1,0:T(8,128)(2,1)S(1)}, u32[]{:S(2)}, u32[]{:S(2)}) %collective-permute-start.11) | collective-permute-done | bytes 442400 | tf_op jit(solution)/shard_map/ppermute | solution.py:30
  46.8 1.6 %shard_map.101 = bf16[512,768]{1,0:T(8,128)(2,1)S(1)} custom-call(s32[1]{0:T(128)} %bitcast.sel, f32[1024,768]{1,0:T(8,128)S(1)} %shard_map.98.acc, bf16[1024,432]{1,0:T(8,128)(2,1)S(1)} %get-tuple-element.60.x0, bf16[1024,432]{1,0:T(8,128)(2,1)S(1)} %get-tuple-element.61.x1, bf16[1024,432]{1,0:T(8,128)(2,1)S(1)} %get-tuple-element.62.x2, ...), custom_call_target="tpu_custom_call" | custom-call | flops 1019215872 | bytes 4194304 | tf_op jit(solution)/shard_map/pallas_call | solution.py:218
  48.7 1.6 %shard_map.100.fk = bf16[512,768]{1,0:T(8,128)(2,1)S(1)} custom-call(s32[1]{0:T(128)} %bitcast.sel, f32[1024,768]{1,0:T(8,128)S(1)} %shard_map.98.acc, bf16[1024,432]{1,0:T(8,128)(2,1)S(1)} %get-tuple-element.60.x0, bf16[1024,432]{1,0:T(8,128)(2,1)S(1)} %get-tuple-element.61.x1, bf16[1024,432]{1,0:T(8,128)(2,1)S(1)} %get-tuple-element.62.x2, ...), custom_call_target="tpu_custom_call" | custom-call | flops 1019215872 | bytes 4194304 | tf_op jit(solution)/shard_map/pallas_call | solution.py:218
  50.9 1.7 %shard_map.102 = (bf16[256,256]{1,0:T(8,128)(2,1)S(1)}, bf16[256,256]{1,0:T(8,128)(2,1)S(1)}, bf16[1280,128]{1,0:T(8,128)(2,1)S(1)}) custom-call(s32[1]{0:T(128)} %bitcast.sel, bf16[512,768]{1,0:T(8,128)(2,1)S(1)} %shard_map.100.fk, bf16[512,768]{1,0:T(8,128)(2,1)S(1)} %collective-permute-done.12.fr, bf16[1536,512]{1,0:T(8,128)(2,1)S(1)} %copy-done.1, ...), custom_call_target="tpu_custom_call" | custom-call | flops 1006632960 | bytes 4194304 | tf_op jit(solution)/shard_map/pallas_call | solution.py:253
  52.8 3.0 %collective-permute-start.14 = (bf16[1280,128]{1,0:T(8,128)(2,1)S(1)}, bf16[1280,128]{1,0:T(8,128)(2,1)S(1)}, u32[]{:S(2)}, u32[]{:S(2)}) collective-permute-start(bf16[1280,128]{1,0:T(8,128)(2,1)S(1)} %get-tuple-element.68.refs_2_), channel_id=1, source_target_pairs={{0,4},{1,13},{16,20},{17,29},{32,36},{33,45},{48,52},{49,61},{2,6}... | collective-permute-start | bytes 983048 | tf_op jit(solution)/shard_map/ppermute | solution.py:30
  57.4 1.7 %shard_map.103 = (f32[1024,128]{1,0:T(8,128)S(1)}, f32[1024,256]{1,0:T(8,128)S(1)}) custom-call(bf16[256,256]{1,0:T(8,128)(2,1)S(1)} %get-tuple-element.66.refs_0_, bf16[256,256]{1,0:T(8,128)(2,1)S(1)} %collective-permute-done.13.refs_1_, bf16[1280,128]{1,0:T(8,128)(2,1)S(1)} %get-tuple-element.68.refs_2_, bf16[1280,128]{1,0:T(8,128)(2,1)S(1)} %collective-permute-done.16.refs_3_), custom_call_target="tpu_custom_call" | custom-call | bytes 1048576 | tf_op jit(solution)/shard_map/pallas_call | solution.py:316
  59.2 3.3 %collective-permute-done.14.refs_2_ = bf16[1280,128]{1,0:T(8,128)(2,1)S(1)} collective-permute-done((bf16[1280,128]{1,0:T(8,128)(2,1)S(1)}, bf16[1280,128]{1,0:T(8,128)(2,1)S(1)}, u32[]{:S(2)}, u32[]{:S(2)}) %collective-permute-start.14) | collective-permute-done | bytes 327712 | tf_op jit(solution)/shard_map/ppermute | solution.py:30
  62.5 1.8 %collective-permute-done.15.refs_3_ = bf16[1280,128]{1,0:T(8,128)(2,1)S(1)} collective-permute-done((bf16[1280,128]{1,0:T(8,128)(2,1)S(1)}, bf16[1280,128]{1,0:T(8,128)(2,1)S(1)}, u32[]{:S(2)}, u32[]{:S(2)}) %collective-permute-start.15) | collective-permute-done | bytes 327712 | tf_op jit(solution)/shard_map/ppermute | solution.py:30
  64.8 2.3 %collective-permute-start.17 = (bf16[1280,128]{1,0:T(8,128)(2,1)S(1)}, bf16[1280,128]{1,0:T(8,128)(2,1)S(1)}, u32[]{:S(2)}, u32[]{:S(2)}) collective-permute-start(bf16[1280,128]{1,0:T(8,128)(2,1)S(1)} %collective-permute-done.14.refs_2_), channel_id=1, source_target_pairs={{0,4},{1,13},{16,20},{17,29},{32,36},{33,45},{48,52},{49,61},{2,6}... | collective-permute-start | bytes 983048 | tf_op jit(solution)/shard_map/ppermute | solution.py:30
  67.1 2.0 %shard_map.104 = (f32[1024,128]{1,0:T(8,128)S(1)}, f32[1024,256]{1,0:T(8,128)S(1)}) custom-call(bf16[256,256]{1,0:T(8,128)(2,1)S(1)} %get-tuple-element.66.refs_0_, bf16[256,256]{1,0:T(8,128)(2,1)S(1)} %collective-permute-done.13.refs_1_, bf16[1280,128]{1,0:T(8,128)(2,1)S(1)} %collective-permute-done.14.refs_2_, ...), custom_call_target="tpu_custom_call" | custom-call | bytes 1048576 | tf_op jit(solution)/shard_map/pallas_call | solution.py:316
  69.1 2.0 %shard_map.105 = (f32[1024,128]{1,0:T(8,128)S(1)}, f32[1024,256]{1,0:T(8,128)S(1)}) custom-call(bf16[256,256]{1,0:T(8,128)(2,1)S(1)} %get-tuple-element.66.refs_0_, bf16[256,256]{1,0:T(8,128)(2,1)S(1)} %collective-permute-done.13.refs_1_, bf16[1280,128]{1,0:T(8,128)(2,1)S(1)} %collective-permute-done.18.refs_2_, ...), custom_call_target="tpu_custom_call" | custom-call | bytes 1048576 | tf_op jit(solution)/shard_map/pallas_call | solution.py:316
  71.2 2.0 %collective-permute-start.20 = (bf16[1280,128]{1,0:T(8,128)(2,1)S(1)}, bf16[1280,128]{1,0:T(8,128)(2,1)S(1)}, u32[]{:S(2)}, u32[]{:S(2)}) collective-permute-start(bf16[1280,128]{1,0:T(8,128)(2,1)S(1)} %collective-permute-done.17.refs_2_), channel_id=1, source_target_pairs={{0,1},{1,0},{16,17},{17,16},{32,33},{33,32},{48,49},{49,48},{2,3},... | collective-permute-start | bytes 983048 | tf_op jit(solution)/shard_map/ppermute | solution.py:30
  74.4 2.1 %shard_map.106.attn = bf16[512,384]{1,0:T(8,128)(2,1)S(1)} custom-call(bf16[256,256]{1,0:T(8,128)(2,1)S(1)} %get-tuple-element.66.refs_0_, bf16[256,256]{1,0:T(8,128)(2,1)S(1)} %collective-permute-done.13.refs_1_, bf16[1280,128]{1,0:T(8,128)(2,1)S(1)} %collective-permute-done.17.refs_2_, bf16[1280,128]{1,0:T(8,128)(2,1)S(1)} %collective-permute-done.20.refs_3_, ...), custom_call_target="tpu_custom_call" | custom-call | bytes 1048576 | tf_op jit(solution)/shard_map/pallas_call | solution.py:316
  76.5 1.7 %shard_map.107 = (f32[384,384]{1,0:T(8,128)S(1)}, bf16[384,384]{1,0:T(8,128)(2,1)S(1)}, bf16[384,384]{1,0:T(8,128)(2,1)S(1)}, bf16[384,384]{1,0:T(8,128)(2,1)S(1)}) custom-call(s32[3]{0:T(128)S(1)} %pad_add_fusion.at, bf16[256,1536]{1,0:T(8,128)(2,1)S(1)} %bitcast.16, bf16[256,1536]{1,0:T(8,128)(2,1)S(1)} %collective-permute-done.21.cot_far, ...), custom_call_target="tpu_custom_call" | custom-call | flops 603979776 | bytes 3145728 | tf_op jit(solution)/shard_map/pallas_call | solution.py:371
  78.8 1.6 %collective-permute-start.24 = (bf16[384,384]{1,0:T(8,128)(2,1)S(1)}, bf16[384,384]{1,0:T(8,128)(2,1)S(1)}, u32[]{:S(2)}, u32[]{:S(2)}) collective-permute-start(bf16[384,384]{1,0:T(8,128)(2,1)S(1)} %get-tuple-element.83), channel_id=1, source_target_pairs={{0,64},{1,5},{16,80},{17,21},{32,96},{33,37},{48,112},{49,53},{2,6... | collective-permute-start | bytes 884744 | tf_op jit(solution)/shard_map/ppermute | solution.py:30
  83.1 1.9 %shard_map.108 = bf16[256,1536]{1,0:T(8,128)(2,1)} custom-call(s32[1]{0:T(128)} %bitcast.sel, bf16[512,768]{1,0:T(8,128)(2,1)S(1)} %shard_map.100.fk, bf16[512,768]{1,0:T(8,128)(2,1)S(1)} %collective-permute-done.12.fr, bf16[512,384]{1,0:T(8,128)(2,1)S(1)} %shard_map.106.attn, bf16[256,384]{1,0:T(8,128)(2,1)S(1)} %collective-permute-done.22.theirs, ...), custom_call_target="tpu_custom_call" | custom-call | flops 603979776 | bytes 4194304 | tf_op jit(solution)/shard_map/pallas_call | solution.py:340
  85.7 3.1 %collective-permute-done.24.b = bf16[384,384]{1,0:T(8,128)(2,1)S(1)} collective-permute-done((bf16[384,384]{1,0:T(8,128)(2,1)S(1)}, bf16[384,384]{1,0:T(8,128)(2,1)S(1)}, u32[]{:S(2)}, u32[]{:S(2)}) %collective-permute-start.24) | collective-permute-done | bytes 294944 | tf_op jit(solution)/shard_map/ppermute | solution.py:30
  89.6 21.0 %all_to_all.5.came = bf16[32,12,384]{2,1,0:T(8,128)(2,1)S(1)} all-to-all(bf16[32,12,384]{2,1,0:T(8,128)(2,1)S(1)} %shard_map.109), channel_id=1, replica_groups={{0,16,32,48,2,18,34,50,4,20,36,52,6,22,38,54,8,24,40,56,10,26,42,58,12,..., dimensions={0} | all-to-all | bytes 589824 | tf_op jit(solution)/shard_map/all_to_all | solution.py:514
  (60 shorter events, 15.9 us)
Async XLA Ops:
  0.6 31.4 %copy-start.5 = (bf16[512,768]{1,0:T(8,128)(2,1)S(1)}, bf16[512,768]{1,0:T(8,128)(2,1)}, u32[]{:S(2)}) copy-start(bf16[512,768]{1,0:T(8,128)(2,1)} %sw_ref.1) | copy-start | bytes 2359300
  0.6 21.2 %collective-permute-start.3 = (bf16[144,1536]{1,0:T(8,128)(2,1)}, bf16[144,1536]{1,0:T(8,128)(2,1)S(1)}, u32[]{:S(2)}, u32[]{:S(2)}) collective-permute-start(bf16[144,1536]{1,0:T(8,128)(2,1)} %bitcast.11), channel_id=1, source_target_pairs={{0,64},{1,17},{16,80},{17,33},{32,96},{33,49},{48,112},{49,3},{2,6... | collective-permute-start | bytes 1327112 | tf_op jit(solution)/shard_map/ppermute | solution.py:30
  3.2 18.7 %collective-permute-start.4 = (bf16[144,1536]{1,0:T(8,128)(2,1)}, bf16[144,1536]{1,0:T(8,128)(2,1)S(1)}, u32[]{:S(2)}, u32[]{:S(2)}) collective-permute-start(bf16[144,1536]{1,0:T(8,128)(2,1)} %bitcast.12), channel_id=1, source_target_pairs={{0,128},{1,33},{16,144},{17,51},{32,160},{33,3},{48,176},{49,17},{... | collective-permute-start | bytes 1327112 | tf_op jit(solution)/shard_map/ppermute | solution.py:30
  6.2 15.7 %collective-permute-start.5 = (bf16[144,1536]{1,0:T(8,128)(2,1)}, bf16[144,1536]{1,0:T(8,128)(2,1)S(1)}, u32[]{:S(2)}, u32[]{:S(2)}) collective-permute-start(bf16[144,1536]{1,0:T(8,128)(2,1)} %bitcast.13), channel_id=1, source_target_pairs={{0,192},{1,51},{16,208},{17,1},{32,224},{33,17},{48,240},{49,33},{... | collective-permute-start | bytes 1327112 | tf_op jit(solution)/shard_map/ppermute | solution.py:30
  10.5 4.1 %collective-permute-start = (bf16[16,128]{1,0:T(8,128)(2,1)S(1)}, bf16[16,128]{1,0:T(8,128)(2,1)S(1)}, u32[]{:S(2)}, u32[]{:S(2)}) collective-permute-start(bf16[16,128]{1,0:T(8,128)(2,1)S(1)} %slice_select_fusion), channel_id=1, source_target_pairs={{0,12},{1,5},{16,28},{17,21},{32,44},{33,37},{48,60},{49,53},{2,14... | collective-permute-start | bytes 12296 | tf_op jit(solution)/shard_map/ppermute | solution.py:30
  14.6 7.1 %collective-permute-start.1 = (bf16[272,128]{1,0:T(8,128)(2,1)S(1)}, bf16[272,128]{1,0:T(8,128)(2,1)S(1)}, u32[]{:S(2)}, u32[]{:S(2)}) collective-permute-start(bf16[272,128]{1,0:T(8,128)(2,1)S(1)} %pad_maximum_fusion.ids_ref), channel_id=1, source_target_pairs={{0,2},{1,3},{16,18},{17,19},{32,34},{33,35},{48,50},{49,51},{2,0},... | collective-permute-start | bytes 208904 | tf_op jit(solution)/shard_map/ppermute | solution.py:30
  16.7 5.2 %collective-permute-start.2 = (bf16[272,128]{1,0:T(8,128)(2,1)S(1)}, bf16[272,128]{1,0:T(8,128)(2,1)S(1)}, u32[]{:S(2)}, u32[]{:S(2)}) collective-permute-start(bf16[272,128]{1,0:T(8,128)(2,1)S(1)} %pad_maximum_fusion.ids_ref), channel_id=1, source_target_pairs={{0,1},{1,0},{16,17},{17,16},{32,33},{33,32},{48,49},{49,48},{2,3},... | collective-permute-start | bytes 208904 | tf_op jit(solution)/shard_map/ppermute | solution.py:30
  21.9 3.7 %collective-permute-start.6 = (bf16[576,768]{1,0:T(8,128)(2,1)S(1)}, bf16[576,768]{1,0:T(8,128)(2,1)S(1)}, u32[]{:S(2)}, u32[]{:S(2)}) collective-permute-start(bf16[576,768]{1,0:T(8,128)(2,1)S(1)} %shard_map.95), channel_id=1, source_target_pairs={{0,1},{1,0},{16,17},{17,16},{32,33},{33,32},{48,49},{49,48},{2,3},... | collective-permute-start | bytes 2654216 | tf_op jit(solution)/shard_map/ppermute | solution.py:30
  25.7 19.0 %collective-permute-start.7 = (bf16[576,768]{1,0:T(8,128)(2,1)S(1)}, bf16[576,768]{1,0:T(8,128)(2,1)S(1)}, u32[]{:S(2)}, u32[]{:S(2)}) collective-permute-start(bf16[576,768]{1,0:T(8,128)(2,1)S(1)} %collective-permute-done.6.refs_0_.r), channel_id=1, source_target_pairs={{0,64},{1,17},{16,80},{17,33},{32,96},{33,49},{48,112},{49,3},{2,6... | collective-permute-start | bytes 2654216 | tf_op jit(solution)/shard_map/ppermute | solution.py:30
  28.6 16.1 %collective-permute-start.8 = (bf16[576,768]{1,0:T(8,128)(2,1)S(1)}, bf16[576,768]{1,0:T(8,128)(2,1)S(1)}, u32[]{:S(2)}, u32[]{:S(2)}) collective-permute-start(bf16[576,768]{1,0:T(8,128)(2,1)S(1)} %collective-permute-done.6.refs_0_.r), channel_id=1, source_target_pairs={{0,192},{1,51},{16,208},{17,1},{32,224},{33,17},{48,240},{49,33},{... | collective-permute-start | bytes 2654216 | tf_op jit(solution)/shard_map/ppermute | solution.py:30
  30.7 1.3 %collective-permute-start.10 = (bf16[272,128]{1,0:T(8,128)(2,1)S(1)}, bf16[272,128]{1,0:T(8,128)(2,1)S(1)}, u32[]{:S(2)}, u32[]{:S(2)}) collective-permute-start(bf16[272,128]{1,0:T(8,128)(2,1)S(1)} %collective-permute-done.1.far_ref), channel_id=1, source_target_pairs={{0,1},{1,0},{16,17},{17,16},{32,33},{33,32},{48,49},{49,48},{2,3},... | collective-permute-start | bytes 208904 | tf_op jit(solution)/shard_map/ppermute | solution.py:30
  30.7 5.0 %copy-start.3 = (bf16[3,48,1536]{2,1,0:T(8,128)(2,1)S(1)}, bf16[3,48,1536]{2,1,0:T(8,128)(2,1)}, u32[]{:S(2)}) copy-start(bf16[3,48,1536]{2,1,0:T(8,128)(2,1)} %param.10) | copy-start | bytes 1327108
  30.8 13.9 %collective-permute-start.9 = (bf16[144,768]{1,0:T(8,128)(2,1)S(1)}, bf16[144,768]{1,0:T(8,128)(2,1)S(1)}, u32[]{:S(2)}, u32[]{:S(2)}) collective-permute-start(bf16[144,768]{1,0:T(8,128)(2,1)S(1)} %shard_map.96), channel_id=1, source_target_pairs={{0,128},{1,33},{16,144},{17,51},{32,160},{33,3},{48,176},{49,17},{... | collective-permute-start | bytes 663560 | tf_op jit(solution)/shard_map/ppermute | solution.py:30
  44.7 2.1 %collective-permute-start.11 = (bf16[288,768]{1,0:T(8,128)(2,1)S(1)}, bf16[288,768]{1,0:T(8,128)(2,1)S(1)}, u32[]{:S(2)}, u32[]{:S(2)}) collective-permute-start(bf16[288,768]{1,0:T(8,128)(2,1)S(1)} %shard_map.99), channel_id=1, source_target_pairs={{0,1},{1,0},{16,17},{17,16},{32,33},{33,32},{48,49},{49,48},{2,3},... | collective-permute-start | bytes 1327112 | tf_op jit(solution)/shard_map/ppermute | solution.py:30
  48.4 2.4 %copy-start.1 = (bf16[1536,512]{1,0:T(8,128)(2,1)S(1)}, bf16[1536,512]{1,0:T(8,128)(2,1)}, u32[]{:S(2)}) copy-start(bf16[1536,512]{1,0:T(8,128)(2,1)} %wq.1) | copy-start | bytes 4718596
  48.5 2.4 %collective-permute-start.12 = (bf16[512,768]{1,0:T(8,128)(2,1)S(1)}, bf16[512,768]{1,0:T(8,128)(2,1)S(1)}, u32[]{:S(2)}, u32[]{:S(2)}) collective-permute-start(bf16[512,768]{1,0:T(8,128)(2,1)S(1)} %shard_map.101), channel_id=1, source_target_pairs={{0,1},{1,0},{16,17},{17,16},{32,33},{33,32},{48,49},{49,48},{2,3},... | collective-permute-start | bytes 2359304 | tf_op jit(solution)/shard_map/ppermute | solution.py:30
  50.4 6.1 %copy-start.6 = (bf16[1,256,1536]{2,1,0:T(8,128)(2,1)S(1)}, bf16[1,256,1536]{2,1,0:T(8,128)(2,1)}, u32[]{:S(2)}) copy-start(bf16[1,256,1536]{2,1,0:T(8,128)(2,1)} %param.15) | copy-start | bytes 2359300
  52.5 4.9 %collective-permute-start.16 = (bf16[1280,128]{1,0:T(8,128)(2,1)S(1)}, bf16[1280,128]{1,0:T(8,128)(2,1)S(1)}, u32[]{:S(2)}, u32[]{:S(2)}) collective-permute-start(bf16[1280,128]{1,0:T(8,128)(2,1)S(1)} %get-tuple-element.68.refs_2_), channel_id=1, source_target_pairs={{0,1},{1,0},{16,17},{17,16},{32,33},{33,32},{48,49},{49,48},{2,3},... | collective-permute-start | bytes 983048 | tf_op jit(solution)/shard_map/ppermute | solution.py:30
  52.8 9.8 %collective-permute-start.14 = (bf16[1280,128]{1,0:T(8,128)(2,1)S(1)}, bf16[1280,128]{1,0:T(8,128)(2,1)S(1)}, u32[]{:S(2)}, u32[]{:S(2)}) collective-permute-start(bf16[1280,128]{1,0:T(8,128)(2,1)S(1)} %get-tuple-element.68.refs_2_), channel_id=1, source_target_pairs={{0,4},{1,13},{16,20},{17,29},{32,36},{33,45},{48,52},{49,61},{2,6}... | collective-permute-start | bytes 983048 | tf_op jit(solution)/shard_map/ppermute | solution.py:30
  55.8 8.5 %collective-permute-start.15 = (bf16[1280,128]{1,0:T(8,128)(2,1)S(1)}, bf16[1280,128]{1,0:T(8,128)(2,1)S(1)}, u32[]{:S(2)}, u32[]{:S(2)}) collective-permute-start(bf16[1280,128]{1,0:T(8,128)(2,1)S(1)} %get-tuple-element.68.refs_2_), channel_id=1, source_target_pairs={{0,12},{1,5},{16,28},{17,21},{32,44},{33,37},{48,60},{49,53},{2,14... | collective-permute-start | bytes 983048 | tf_op jit(solution)/shard_map/ppermute | solution.py:30
  55.8 1.6 %collective-permute-start.13 = (bf16[256,256]{1,0:T(8,128)(2,1)S(1)}, bf16[256,256]{1,0:T(8,128)(2,1)S(1)}, u32[]{:S(2)}, u32[]{:S(2)}) collective-permute-start(bf16[256,256]{1,0:T(8,128)(2,1)S(1)} %get-tuple-element.67), channel_id=1, source_target_pairs={{0,1},{1,0},{16,17},{17,16},{32,33},{33,32},{48,49},{49,48},{2,3},... | collective-permute-start | bytes 393224 | tf_op jit(solution)/shard_map/ppermute | solution.py:30
  56.4 20.0 %collective-permute-start.21 = (bf16[256,1536]{1,0:T(8,128)(2,1)S(1)}, bf16[256,1536]{1,0:T(8,128)(2,1)S(1)}, u32[]{:S(2)}, u32[]{:S(2)}) collective-permute-start(bf16[256,1536]{1,0:T(8,128)(2,1)S(1)} %bitcast.15), channel_id=1, source_target_pairs={{0,1},{1,0},{16,17},{17,16},{32,33},{33,32},{48,49},{49,48},{2,3},... | collective-permute-start | bytes 2359304 | tf_op jit(solution)/shard_map/ppermute | solution.py:30
  64.3 4.8 %collective-permute-start.18 = (bf16[1280,128]{1,0:T(8,128)(2,1)S(1)}, bf16[1280,128]{1,0:T(8,128)(2,1)S(1)}, u32[]{:S(2)}, u32[]{:S(2)}) collective-permute-start(bf16[1280,128]{1,0:T(8,128)(2,1)S(1)} %collective-permute-done.14.refs_2_), channel_id=1, source_target_pairs={{0,1},{1,0},{16,17},{17,16},{32,33},{33,32},{48,49},{49,48},{2,3},... | collective-permute-start | bytes 983048 | tf_op jit(solution)/shard_map/ppermute | solution.py:30
  64.3 4.8 %collective-permute-start.19 = (bf16[1280,128]{1,0:T(8,128)(2,1)S(1)}, bf16[1280,128]{1,0:T(8,128)(2,1)S(1)}, u32[]{:S(2)}, u32[]{:S(2)}) collective-permute-start(bf16[1280,128]{1,0:T(8,128)(2,1)S(1)} %collective-permute-done.15.refs_3_), channel_id=1, source_target_pairs={{0,1},{1,0},{16,17},{17,16},{32,33},{33,32},{48,49},{49,48},{2,3},... | collective-permute-start | bytes 983048 | tf_op jit(solution)/shard_map/ppermute | solution.py:30
  64.8 6.3 %collective-permute-start.17 = (bf16[1280,128]{1,0:T(8,128)(2,1)S(1)}, bf16[1280,128]{1,0:T(8,128)(2,1)S(1)}, u32[]{:S(2)}, u32[]{:S(2)}) collective-permute-start(bf16[1280,128]{1,0:T(8,128)(2,1)S(1)} %collective-permute-done.14.refs_2_), channel_id=1, source_target_pairs={{0,4},{1,13},{16,20},{17,29},{32,36},{33,45},{48,52},{49,61},{2,6}... | collective-permute-start | bytes 983048 | tf_op jit(solution)/shard_map/ppermute | solution.py:30
  71.2 12.0 %copy-start = (bf16[1536,768]{1,0:T(8,128)(2,1)S(1)}, bf16[1536,768]{1,0:T(8,128)(2,1)}, u32[]{:S(2)}) copy-start(bf16[1536,768]{1,0:T(8,128)(2,1)} %w.1) | copy-start | bytes 7077892
  71.2 3.2 %collective-permute-start.20 = (bf16[1280,128]{1,0:T(8,128)(2,1)S(1)}, bf16[1280,128]{1,0:T(8,128)(2,1)S(1)}, u32[]{:S(2)}, u32[]{:S(2)}) collective-permute-start(bf16[1280,128]{1,0:T(8,128)(2,1)S(1)} %collective-permute-done.17.refs_2_), channel_id=1, source_target_pairs={{0,1},{1,0},{16,17},{17,16},{32,33},{33,32},{48,49},{49,48},{2,3},... | collective-permute-start | bytes 983048 | tf_op jit(solution)/shard_map/ppermute | solution.py:30
  78.2 7.5 %collective-permute-start.23 = (bf16[384,384]{1,0:T(8,128)(2,1)S(1)}, bf16[384,384]{1,0:T(8,128)(2,1)S(1)}, u32[]{:S(2)}, u32[]{:S(2)}) collective-permute-start(bf16[384,384]{1,0:T(8,128)(2,1)S(1)} %get-tuple-element.85), channel_id=1, source_target_pairs={{0,128},{1,9},{16,144},{17,25},{32,160},{33,41},{48,176},{49,57},{... | collective-permute-start | bytes 884744 | tf_op jit(solution)/shard_map/ppermute | solution.py:30
  78.8 9.9 %collective-permute-start.24 = (bf16[384,384]{1,0:T(8,128)(2,1)S(1)}, bf16[384,384]{1,0:T(8,128)(2,1)S(1)}, u32[]{:S(2)}, u32[]{:S(2)}) collective-permute-start(bf16[384,384]{1,0:T(8,128)(2,1)S(1)} %get-tuple-element.83), channel_id=1, source_target_pairs={{0,64},{1,5},{16,80},{17,21},{32,96},{33,37},{48,112},{49,53},{2,6... | collective-permute-start | bytes 884744 | tf_op jit(solution)/shard_map/ppermute | solution.py:30
  80.4 8.4 %collective-permute-start.25 = (bf16[384,384]{1,0:T(8,128)(2,1)S(1)}, bf16[384,384]{1,0:T(8,128)(2,1)S(1)}, u32[]{:S(2)}, u32[]{:S(2)}) collective-permute-start(bf16[384,384]{1,0:T(8,128)(2,1)S(1)} %get-tuple-element.86), channel_id=1, source_target_pairs={{0,192},{1,13},{16,208},{17,29},{32,224},{33,45},{48,240},{49,61},... | collective-permute-start | bytes 884744 | tf_op jit(solution)/shard_map/ppermute | solution.py:30
  81.5 1.6 %collective-permute-start.22 = (bf16[256,384]{1,0:T(8,128)(2,1)S(1)}, bf16[256,384]{1,0:T(8,128)(2,1)S(1)}, u32[]{:S(2)}, u32[]{:S(2)}) collective-permute-start(bf16[256,384]{1,0:T(8,128)(2,1)S(1)} %slice.11), channel_id=1, source_target_pairs={{0,1},{1,0},{16,17},{17,16},{32,33},{33,32},{48,49},{49,48},{2,3},... | collective-permute-start | bytes 589832 | tf_op jit(solution)/shard_map/ppermute | solution.py:30
  110.6 2.0 %collective-permute-start.26 = (f32[6,384]{1,0:T(8,128)S(1)}, f32[6,384]{1,0:T(8,128)S(1)}, u32[]{:S(2)}, u32[]{:S(2)}) collective-permute-start(f32[6,384]{1,0:T(8,128)S(1)} %get-tuple-element.93), channel_id=1, source_target_pairs={{0,1},{1,0},{16,17},{17,16},{32,33},{33,32},{48,49},{49,48},{2,3},... | collective-permute-start | bytes 27656 | tf_op jit(solution)/shard_map/ppermute | solution.py:30
  (2 other events, 4.8 us)
where the time goes:
time: 113 us
  starting transfers between devices  38.3 us (34%)
  waiting for transfers between devices  26.7 us (24%)
  Pallas kernels  24.9 us (22%)
  blocking collectives  21 us (19%)
  other arithmetic  1.37 us (1%)
    ppermute x27, starting transfers between devices, route(): return lax.ppermute(value, ('dp', 'seq'), pairs)  38.3 us
    ppermute x27, waiting for transfers between devices, route(): return lax.ppermute(value, ('dp', 'seq'), pairs)  26.7 us
    all_to_all x1, blocking collectives, local(): came = lax.all_to_all(chunks, ('dp', 'seq'), 0, 0, axis_index_groups=groups)  21 us
    pallas_call x4, Pallas kernels, attend(): pl.pallas_call(functools.partial(attend_kernel, tuple((len(g) for g in kv...  7.76 us
    pallas_call x1, Pallas kernels, local(): pl.pallas_call(stem_kernel, in_specs=[SMEM] + [VMEM] * 5, out_shape=[shap...  3.78 us
    pallas_call x2, Pallas kernels, conv2(): pl.pallas_call(functools.partial(conv2_kernel, part), in_specs=[SMEM] + [...  3.28 us
    pallas_call x1, Pallas kernels, conv1(): pl.pallas_call(conv1_kernel, in_specs=[SMEM] + [VMEM] * 8, out_shape=shap...  3.2 us
  transfers between devices with their start and end apart: 27, of which 15 were waited for; matrix products, arithmetic and copies ran while one was open for 1% of the time, Pallas kernels for 16%

commit v1 on v0

--- a/solution.py
+++ b/solution.py
@@ -224,7 +224,7 @@
     )(c, acc, *xs, *pieces)
 
 
-def project_kernel(sel, fk, fr, wq, wk, wv, q_mine, q_send, kv_out):
+def project_kernel(sel, fk, fr, wq, wk, wv, q_mine, message, kv_out):
     n_pos, half, qc = fk.shape[0] // 2, fk.shape[1], wq.shape[1] // 2
     c = sel[0]
     my, other = [pl.ds(pl.multiple_of(k * half, half), half) for k in (c, 1 - c)]
@@ -236,7 +236,10 @@
     nk, nr = (wide_k * scale).astype(BF), (wide_r * scale).astype(BF)
     factor = HQK ** (-0.5) * math.log2(math.e)
     hk, hr = nk[:n_pos], nr[:n_pos]
-    q_send[...] = ((dot(hk, wq[my, theirs]) + dot(hr, wq[other, theirs])) * factor).astype(BF)
+    q = ((dot(hk, wq[my, theirs]) + dot(hr, wq[other, theirs])) * factor).astype(BF)
+    for h in range(qc // HQK):
+        at = (5 + h) * n_pos
+        message[at : at + n_pos, :] = q[:, h * HQK : (h + 1) * HQK]
     q_mine[...] = ((dot(hk, wq[my, mine]) + dot(hr, wq[other, mine])) * factor).astype(BF)
     n = 2 * n_pos
     kv_out[:n, :] = (dot(nk, wk[my, :]) + dot(nr, wk[other, :])).astype(BF)
@@ -244,6 +247,7 @@
     kv_out[n : 2 * n, :] = v[:, :128].astype(BF)
     tail = v[:, 128:]
     kv_out[2 * n :, :] = jnp.concatenate([tail[:n_pos], tail[n_pos:]], axis=1).astype(BF)
+    message[: 5 * n_pos, :] = kv_out[...]
 
 
 def project(c, f_keep, f_recv, query_weight, key_weight, value_weight):
@@ -253,7 +257,7 @@
     return pl.pallas_call(
         project_kernel,
         in_specs=[SMEM] + [VMEM] * 5,
-        out_shape=[shape(n_pos, qc), shape(n_pos, qc), shape(5 * n_pos, 128)],
+        out_shape=[shape(n_pos, qc), shape(7 * n_pos, 128), shape(5 * n_pos, 128)],
         compiler_params=params(),
         cost_estimate=cost(4 * n * half * 640, 4 << 20),
     )(c, f_keep, f_recv, query_weight, key_weight, value_weight)
@@ -274,7 +278,7 @@
     at = 2
     kvs = []
     for n in groups:
-        kvs.append(unpack(jnp.concatenate([r[...] for r in refs[at : at + n]])))
+        kvs.append(unpack(refs[at][: 5 * qs[0].shape[0], :]))
         at += n
     rest = refs[at:]
     if not first:
@@ -283,7 +287,10 @@
     rows = qs[0].shape[0]
     for w in range(2):
         for h in range(HEADS // 2):
-            q = qs[w][:, h * HQK : (h + 1) * HQK]
+            if w == 0:
+                q = qs[0][:, h * HQK : (h + 1) * HQK]
+            else:
+                q = qs[1][(5 + h) * rows : (6 + h) * rows, :]
             scores = [dot_t(q, k) for k, _ in kvs]
             top = functools.reduce(
                 jnp.maximum, [jnp.max(s, axis=1, keepdims=True) for s in scores]
@@ -489,11 +496,11 @@
     pieces = [b1, b3, send(pick(core, [b1, b3], 3 * share, True), dc=1), last]
     f_recv = send(conv2(core, acc, xs[3:], pieces, 0), dc=1)
     f_keep = conv2(core, acc, xs[3:], pieces, 1)
-    q_mine, q_send, kv = project(core, f_keep, f_recv, query_weight, key_weight, value_weight.T)
+    q_mine, message, kv = project(core, f_keep, f_recv, query_weight, key_weight, value_weight.T)
 
     r1, r2 = round_ring(kv), round_ring(kv, -1)
-    qs = [q_mine, send(q_send, dc=1)]
-    state = attend(qs, [[kv], [send(kv, dc=1)]], (), False)
+    qs = [q_mine, send(message, dc=1)]
+    state = attend(qs, [[kv], [qs[1]]], (), False)
     r1, r2, *state = lax.optimization_barrier((r1, r2, *state))
     rr = round_ring(r1)
     r1_o, r2_o = send(r1, dc=1), send(r2, dc=1)

time: 113 us -> 113 us (level)
    ppermute x27 -> x26, waiting for transfers between devices: 26.7 us -> 26.9 us  [route(): return lax.ppermute(value, ('dp', 'seq'), pairs)]
    ppermute x27 -> x26, starting transfers between devices: 38.3 us -> 38.3 us  [route(): return lax.ppermute(value, ('dp', 'seq'), pairs)]
  transfers between devices with their start and end apart: 27 -> 26, of which waited for: 15 -> 15; matrix products, arithmetic and copies ran while one was open for 1% -> 1% of each run, Pallas kernels for 16% -> 16%
where the time goes in v1:
time: 113 us
  starting transfers between devices  38.3 us (34%)
  waiting for transfers between devices  26.9 us (24%)
  Pallas kernels  24.8 us (22%)
  blocking collectives  20.9 us (18%)
  other arithmetic  1.37 us (1%)
    ppermute x26, starting transfers between devices, route(): return lax.ppermute(value, ('dp', 'seq'), pairs)  38.3 us
    ppermute x26, waiting for transfers between devices, route(): return lax.ppermute(value, ('dp', 'seq'), pairs)  26.9 us
    all_to_all x1, blocking collectives, local(): came = lax.all_to_all(chunks, ('dp', 'seq'), 0, 0, axis_index_groups=groups)  20.9 us
    pallas_call x4, Pallas kernels, attend(): pl.pallas_call(functools.partial(attend_kernel, tuple((len(g) for g in kv...  7.53 us
    pallas_call x1, Pallas kernels, local(): pl.pallas_call(stem_kernel, in_specs=[SMEM] + [VMEM] * 5, out_shape=[shap...  3.78 us
    pallas_call x2, Pallas kernels, conv2(): pl.pallas_call(functools.partial(conv2_kernel, part), in_specs=[SMEM] + [...  3.28 us
    pallas_call x1, Pallas kernels, conv1(): pl.pallas_call(conv1_kernel, in_specs=[SMEM] + [VMEM] * 8, out_shape=shap...  3.2 us
  transfers between devices with their start and end apart: 26, of which 15 were waited for; matrix products, arithmetic and copies ran while one was open for 1% of the time, Pallas kernels for 16%

profile of v1, /device:TPU:1, one launch (start us, length us, event | category | flops | bytes accessed | tf_op | source)
XLA Modules:
  0.0 113.3 jit_solution(13785078006092371138)
XLA Ops:
  0.6 2.5 %collective-permute-start.3 = (bf16[144,1536]{1,0:T(8,128)(2,1)}, bf16[144,1536]{1,0:T(8,128)(2,1)S(1)}, u32[]{:S(2)}, u32[]{:S(2)}) collective-permute-start(bf16[144,1536]{1,0:T(8,128)(2,1)} %bitcast.11), channel_id=1, source_target_pairs={{0,64},{1,17},{16,80},{17,33},{32,96},{33,49},{48,112},{49,3},{2,6... | collective-permute-start | bytes 1327112 | tf_op jit(solution)/shard_map/ppermute | solution.py:30
  3.2 3.0 %collective-permute-start.4 = (bf16[144,1536]{1,0:T(8,128)(2,1)}, bf16[144,1536]{1,0:T(8,128)(2,1)S(1)}, u32[]{:S(2)}, u32[]{:S(2)}) collective-permute-start(bf16[144,1536]{1,0:T(8,128)(2,1)} %bitcast.12), channel_id=1, source_target_pairs={{0,128},{1,33},{16,144},{17,51},{32,160},{33,3},{48,176},{49,17},{... | collective-permute-start | bytes 1327112 | tf_op jit(solution)/shard_map/ppermute | solution.py:30
  6.2 2.9 %collective-permute-start.5 = (bf16[144,1536]{1,0:T(8,128)(2,1)}, bf16[144,1536]{1,0:T(8,128)(2,1)S(1)}, u32[]{:S(2)}, u32[]{:S(2)}) collective-permute-start(bf16[144,1536]{1,0:T(8,128)(2,1)} %bitcast.13), channel_id=1, source_target_pairs={{0,192},{1,51},{16,208},{17,1},{32,224},{33,17},{48,240},{49,33},{... | collective-permute-start | bytes 1327112 | tf_op jit(solution)/shard_map/ppermute | solution.py:30
  10.5 1.4 %collective-permute-start = (bf16[16,128]{1,0:T(8,128)(2,1)S(1)}, bf16[16,128]{1,0:T(8,128)(2,1)S(1)}, u32[]{:S(2)}, u32[]{:S(2)}) collective-permute-start(bf16[16,128]{1,0:T(8,128)(2,1)S(1)} %slice_select_fusion), channel_id=1, source_target_pairs={{0,12},{1,5},{16,28},{17,21},{32,44},{33,37},{48,60},{49,53},{2,14... | collective-permute-start | bytes 12296 | tf_op jit(solution)/shard_map/ppermute | solution.py:30
  11.9 2.7 %collective-permute-done = bf16[16,128]{1,0:T(8,128)(2,1)S(1)} collective-permute-done((bf16[16,128]{1,0:T(8,128)(2,1)S(1)}, bf16[16,128]{1,0:T(8,128)(2,1)S(1)}, u32[]{:S(2)}, u32[]{:S(2)}) %collective-permute-start) | collective-permute-done | bytes 4128 | tf_op jit(solution)/shard_map/ppermute | solution.py:30
  14.6 2.1 %collective-permute-start.1 = (bf16[272,128]{1,0:T(8,128)(2,1)S(1)}, bf16[272,128]{1,0:T(8,128)(2,1)S(1)}, u32[]{:S(2)}, u32[]{:S(2)}) collective-permute-start(bf16[272,128]{1,0:T(8,128)(2,1)S(1)} %pad_maximum_fusion.ids_ref), channel_id=1, source_target_pairs={{0,2},{1,3},{16,18},{17,19},{32,34},{33,35},{48,50},{49,51},{2,0},... | collective-permute-start | bytes 208904 | tf_op jit(solution)/shard_map/ppermute | solution.py:30
  16.7 4.2 %collective-permute-start.2 = (bf16[272,128]{1,0:T(8,128)(2,1)S(1)}, bf16[272,128]{1,0:T(8,128)(2,1)S(1)}, u32[]{:S(2)}, u32[]{:S(2)}) collective-permute-start(bf16[272,128]{1,0:T(8,128)(2,1)S(1)} %pad_maximum_fusion.ids_ref), channel_id=1, source_target_pairs={{0,1},{1,0},{16,17},{17,16},{32,33},{33,32},{48,49},{49,48},{2,3},... | collective-permute-start | bytes 208904 | tf_op jit(solution)/shard_map/ppermute | solution.py:30
  21.9 1.7 %collective-permute-start.6 = (bf16[576,768]{1,0:T(8,128)(2,1)S(1)}, bf16[576,768]{1,0:T(8,128)(2,1)S(1)}, u32[]{:S(2)}, u32[]{:S(2)}) collective-permute-start(bf16[576,768]{1,0:T(8,128)(2,1)S(1)} %shard_map.95), channel_id=1, source_target_pairs={{0,1},{1,0},{16,17},{17,16},{32,33},{33,32},{48,49},{49,48},{2,3},... | collective-permute-start | bytes 2654216 | tf_op jit(solution)/shard_map/ppermute | solution.py:30
  23.6 2.1 %collective-permute-done.6.refs_0_.r = bf16[576,768]{1,0:T(8,128)(2,1)S(1)} collective-permute-done((bf16[576,768]{1,0:T(8,128)(2,1)S(1)}, bf16[576,768]{1,0:T(8,128)(2,1)S(1)}, u32[]{:S(2)}, u32[]{:S(2)}) %collective-permute-start.6) | collective-permute-done | bytes 884768 | tf_op jit(solution)/shard_map/ppermute | solution.py:30
  25.7 2.9 %collective-permute-start.7 = (bf16[576,768]{1,0:T(8,128)(2,1)S(1)}, bf16[576,768]{1,0:T(8,128)(2,1)S(1)}, u32[]{:S(2)}, u32[]{:S(2)}) collective-permute-start(bf16[576,768]{1,0:T(8,128)(2,1)S(1)} %collective-permute-done.6.refs_0_.r), channel_id=1, source_target_pairs={{0,64},{1,17},{16,80},{17,33},{32,96},{33,49},{48,112},{49,3},{2,6... | collective-permute-start | bytes 2654216 | tf_op jit(solution)/shard_map/ppermute | solution.py:30
  28.6 2.1 %collective-permute-start.8 = (bf16[576,768]{1,0:T(8,128)(2,1)S(1)}, bf16[576,768]{1,0:T(8,128)(2,1)S(1)}, u32[]{:S(2)}, u32[]{:S(2)}) collective-permute-start(bf16[576,768]{1,0:T(8,128)(2,1)S(1)} %collective-permute-done.6.refs_0_.r), channel_id=1, source_target_pairs={{0,192},{1,51},{16,208},{17,1},{32,224},{33,17},{48,240},{49,33},{... | collective-permute-start | bytes 2654216 | tf_op jit(solution)/shard_map/ppermute | solution.py:30
  32.0 3.8 %shard_map.97 = (bf16[1024,336]{1,0:T(8,128)(2,1)S(1)}, bf16[1024,336]{1,0:T(8,128)(2,1)S(1)}, bf16[1024,336]{1,0:T(8,128)(2,1)S(1)}, bf16[1024,432]{1,0:T(8,128...) custom-call(s32[5]{0:T(128)S(1)} %stack.26.place, bf16[512,768]{1,0:T(8,128)(2,1)S(1)} %copy-done.5, ...), custom_call_target="tpu_custom_call" | custom-call | flops 4000000000 | bytes 8388608 | tf_op jit(solution)/shard_map/pallas_call | solution.py:479
  35.8 3.2 %shard_map.98.acc = f32[1024,768]{1,0:T(8,128)S(1)} custom-call(s32[1]{0:T(128)} %bitcast.sel, bf16[1024,336]{1,0:T(8,128)(2,1)S(1)} %get-tuple-element.56.x0, bf16[1024,336]{1,0:T(8,128)(2,1)S(1)} %get-tuple-element.57.x1, bf16[1024,336]{1,0:T(8,128)(2,1)S(1)} %get-tuple-element.58.x2, bf16[144,1536]{1,0:T(8,128)(2,1)S(1)} %bitcast.14, ...), custom_call_target="tpu_custom_call" | custom-call | flops 1585446912 | bytes 7340032 | tf_op jit(solution)/shard_map/pallas_call | solution.py:207
  39.0 5.7 %collective-permute-done.9.last = bf16[144,768]{1,0:T(8,128)(2,1)S(1)} collective-permute-done((bf16[144,768]{1,0:T(8,128)(2,1)S(1)}, bf16[144,768]{1,0:T(8,128)(2,1)S(1)}, u32[]{:S(2)}, u32[]{:S(2)}) %collective-permute-start.9) | collective-permute-done | bytes 221216 | tf_op jit(solution)/shard_map/ppermute | solution.py:30
  45.0 1.8 %collective-permute-done.11.swapped = bf16[288,768]{1,0:T(8,128)(2,1)S(1)} collective-permute-done((bf16[288,768]{1,0:T(8,128)(2,1)S(1)}, bf16[288,768]{1,0:T(8,128)(2,1)S(1)}, u32[]{:S(2)}, u32[]{:S(2)}) %collective-permute-start.11) | collective-permute-done | bytes 442400 | tf_op jit(solution)/shard_map/ppermute | solution.py:30
  46.8 1.6 %shard_map.101 = bf16[512,768]{1,0:T(8,128)(2,1)S(1)} custom-call(s32[1]{0:T(128)} %bitcast.sel, f32[1024,768]{1,0:T(8,128)S(1)} %shard_map.98.acc, bf16[1024,432]{1,0:T(8,128)(2,1)S(1)} %get-tuple-element.60.x0, bf16[1024,432]{1,0:T(8,128)(2,1)S(1)} %get-tuple-element.61.x1, bf16[1024,432]{1,0:T(8,128)(2,1)S(1)} %get-tuple-element.62.x2, ...), custom_call_target="tpu_custom_call" | custom-call | flops 1019215872 | bytes 4194304 | tf_op jit(solution)/shard_map/pallas_call | solution.py:218
  48.7 1.6 %shard_map.100.fk = bf16[512,768]{1,0:T(8,128)(2,1)S(1)} custom-call(s32[1]{0:T(128)} %bitcast.sel, f32[1024,768]{1,0:T(8,128)S(1)} %shard_map.98.acc, bf16[1024,432]{1,0:T(8,128)(2,1)S(1)} %get-tuple-element.60.x0, bf16[1024,432]{1,0:T(8,128)(2,1)S(1)} %get-tuple-element.61.x1, bf16[1024,432]{1,0:T(8,128)(2,1)S(1)} %get-tuple-element.62.x2, ...), custom_call_target="tpu_custom_call" | custom-call | flops 1019215872 | bytes 4194304 | tf_op jit(solution)/shard_map/pallas_call | solution.py:218
  50.9 1.7 %shard_map.102 = (bf16[256,256]{1,0:T(8,128)(2,1)S(1)}, bf16[1792,128]{1,0:T(8,128)(2,1)S(1)}, bf16[1280,128]{1,0:T(8,128)(2,1)S(1)}) custom-call(s32[1]{0:T(128)} %bitcast.sel, bf16[512,768]{1,0:T(8,128)(2,1)S(1)} %shard_map.100.fk, bf16[512,768]{1,0:T(8,128)(2,1)S(1)} %collective-permute-done.12.fr, bf16[1536,512]{1,0:T(8,128)(2,1)S(1)} %copy-done.1, ...), custom_call_target="tpu_custom_call" | custom-call | flops 1006632960 | bytes 4194304 | tf_op jit(solution)/shard_map/pallas_call | solution.py:257
  52.8 3.0 %collective-permute-start.14 = (bf16[1280,128]{1,0:T(8,128)(2,1)S(1)}, bf16[1280,128]{1,0:T(8,128)(2,1)S(1)}, u32[]{:S(2)}, u32[]{:S(2)}) collective-permute-start(bf16[1280,128]{1,0:T(8,128)(2,1)S(1)} %get-tuple-element.68.refs_2_), channel_id=1, source_target_pairs={{0,4},{1,13},{16,20},{17,29},{32,36},{33,45},{48,52},{49,61},{2,6}... | collective-permute-start | bytes 983048 | tf_op jit(solution)/shard_map/ppermute | solution.py:30
  56.5 1.7 %shard_map.103 = (f32[1024,128]{1,0:T(8,128)S(1)}, f32[1024,256]{1,0:T(8,128)S(1)}) custom-call(bf16[256,256]{1,0:T(8,128)(2,1)S(1)} %get-tuple-element.66.refs_0_, bf16[1792,128]{1,0:T(8,128)(2,1)S(1)} %collective-permute-done.13.refs_1_.refs_3_, bf16[1280,128]{1,0:T(8,128)(2,1)S(1)} %get-tuple-element.68.refs_2_, ...), custom_call_target="tpu_custom_call" | custom-call | bytes 1048576 | tf_op jit(solution)/shard_map/pallas_call | solution.py:323
  58.3 4.3 %collective-permute-done.14.refs_2_ = bf16[1280,128]{1,0:T(8,128)(2,1)S(1)} collective-permute-done((bf16[1280,128]{1,0:T(8,128)(2,1)S(1)}, bf16[1280,128]{1,0:T(8,128)(2,1)S(1)}, u32[]{:S(2)}, u32[]{:S(2)}) %collective-permute-start.14) | collective-permute-done | bytes 327712 | tf_op jit(solution)/shard_map/ppermute | solution.py:30
  62.6 1.8 %collective-permute-done.15.refs_3_ = bf16[1280,128]{1,0:T(8,128)(2,1)S(1)} collective-permute-done((bf16[1280,128]{1,0:T(8,128)(2,1)S(1)}, bf16[1280,128]{1,0:T(8,128)(2,1)S(1)}, u32[]{:S(2)}, u32[]{:S(2)}) %collective-permute-start.15) | collective-permute-done | bytes 327712 | tf_op jit(solution)/shard_map/ppermute | solution.py:30
  64.9 2.3 %collective-permute-start.16 = (bf16[1280,128]{1,0:T(8,128)(2,1)S(1)}, bf16[1280,128]{1,0:T(8,128)(2,1)S(1)}, u32[]{:S(2)}, u32[]{:S(2)}) collective-permute-start(bf16[1280,128]{1,0:T(8,128)(2,1)S(1)} %collective-permute-done.14.refs_2_), channel_id=1, source_target_pairs={{0,4},{1,13},{16,20},{17,29},{32,36},{33,45},{48,52},{49,61},{2,6}... | collective-permute-start | bytes 983048 | tf_op jit(solution)/shard_map/ppermute | solution.py:30
  67.2 1.9 %shard_map.104 = (f32[1024,128]{1,0:T(8,128)S(1)}, f32[1024,256]{1,0:T(8,128)S(1)}) custom-call(bf16[256,256]{1,0:T(8,128)(2,1)S(1)} %get-tuple-element.66.refs_0_, bf16[1792,128]{1,0:T(8,128)(2,1)S(1)} %collective-permute-done.13.refs_1_.refs_3_, bf16[1280,128]{1,0:T(8,128)(2,1)S(1)} %collective-permute-done.14.refs_2_, ...), custom_call_target="tpu_custom_call" | custom-call | bytes 1048576 | tf_op jit(solution)/shard_map/pallas_call | solution.py:323
  69.1 1.9 %shard_map.105 = (f32[1024,128]{1,0:T(8,128)S(1)}, f32[1024,256]{1,0:T(8,128)S(1)}) custom-call(bf16[256,256]{1,0:T(8,128)(2,1)S(1)} %get-tuple-element.66.refs_0_, bf16[1792,128]{1,0:T(8,128)(2,1)S(1)} %collective-permute-done.13.refs_1_.refs_3_, bf16[1280,128]{1,0:T(8,128)(2,1)S(1)} %collective-permute-done.17.refs_2_, ...), custom_call_target="tpu_custom_call" | custom-call | bytes 1048576 | tf_op jit(solution)/shard_map/pallas_call | solution.py:323
  71.2 2.0 %collective-permute-start.19 = (bf16[1280,128]{1,0:T(8,128)(2,1)S(1)}, bf16[1280,128]{1,0:T(8,128)(2,1)S(1)}, u32[]{:S(2)}, u32[]{:S(2)}) collective-permute-start(bf16[1280,128]{1,0:T(8,128)(2,1)S(1)} %collective-permute-done.16.refs_2_), channel_id=1, source_target_pairs={{0,1},{1,0},{16,17},{17,16},{32,33},{33,32},{48,49},{49,48},{2,3},... | collective-permute-start | bytes 983048 | tf_op jit(solution)/shard_map/ppermute | solution.py:30
  74.5 2.0 %shard_map.106.attn = bf16[512,384]{1,0:T(8,128)(2,1)S(1)} custom-call(bf16[256,256]{1,0:T(8,128)(2,1)S(1)} %get-tuple-element.66.refs_0_, bf16[1792,128]{1,0:T(8,128)(2,1)S(1)} %collective-permute-done.13.refs_1_.refs_3_, bf16[1280,128]{1,0:T(8,128)(2,1)S(1)} %collective-permute-done.16.refs_2_, bf16[1280,128]{1,0:T(8,128)(2,1)S(1)} %collective-permute-done.19.refs_3_, ...), custom_call_target="tpu_custom_call" | custom-call | bytes 1048576 | tf_op jit(solution)/shard_map/pallas_call | solution.py:323
  76.5 1.7 %shard_map.107 = (f32[384,384]{1,0:T(8,128)S(1)}, bf16[384,384]{1,0:T(8,128)(2,1)S(1)}, bf16[384,384]{1,0:T(8,128)(2,1)S(1)}, bf16[384,384]{1,0:T(8,128)(2,1)S(1)}) custom-call(s32[3]{0:T(128)S(1)} %pad_add_fusion.at, bf16[256,1536]{1,0:T(8,128)(2,1)S(1)} %bitcast.16, bf16[256,1536]{1,0:T(8,128)(2,1)S(1)} %collective-permute-done.20.cot_far, ...), custom_call_target="tpu_custom_call" | custom-call | flops 603979776 | bytes 3145728 | tf_op jit(solution)/shard_map/pallas_call | solution.py:378
  78.8 1.6 %collective-permute-start.23 = (bf16[384,384]{1,0:T(8,128)(2,1)S(1)}, bf16[384,384]{1,0:T(8,128)(2,1)S(1)}, u32[]{:S(2)}, u32[]{:S(2)}) collective-permute-start(bf16[384,384]{1,0:T(8,128)(2,1)S(1)} %get-tuple-element.83), channel_id=1, source_target_pairs={{0,64},{1,5},{16,80},{17,21},{32,96},{33,37},{48,112},{49,53},{2,6... | collective-permute-start | bytes 884744 | tf_op jit(solution)/shard_map/ppermute | solution.py:30
  83.2 1.9 %shard_map.108 = bf16[256,1536]{1,0:T(8,128)(2,1)} custom-call(s32[1]{0:T(128)} %bitcast.sel, bf16[512,768]{1,0:T(8,128)(2,1)S(1)} %shard_map.100.fk, bf16[512,768]{1,0:T(8,128)(2,1)S(1)} %collective-permute-done.12.fr, bf16[512,384]{1,0:T(8,128)(2,1)S(1)} %shard_map.106.attn, bf16[256,384]{1,0:T(8,128)(2,1)S(1)} %collective-permute-done.21.theirs, ...), custom_call_target="tpu_custom_call" | custom-call | flops 603979776 | bytes 4194304 | tf_op jit(solution)/shard_map/pallas_call | solution.py:347
  85.7 3.1 %collective-permute-done.23.b = bf16[384,384]{1,0:T(8,128)(2,1)S(1)} collective-permute-done((bf16[384,384]{1,0:T(8,128)(2,1)S(1)}, bf16[384,384]{1,0:T(8,128)(2,1)S(1)}, u32[]{:S(2)}, u32[]{:S(2)}) %collective-permute-start.23) | collective-permute-done | bytes 294944 | tf_op jit(solution)/shard_map/ppermute | solution.py:30
  89.6 20.9 %all_to_all.5.came = bf16[32,12,384]{2,1,0:T(8,128)(2,1)S(1)} all-to-all(bf16[32,12,384]{2,1,0:T(8,128)(2,1)S(1)} %shard_map.109), channel_id=1, replica_groups={{0,16,32,48,2,18,34,50,4,20,36,52,6,22,38,54,8,24,40,56,10,26,42,58,12,..., dimensions={0} | all-to-all | bytes 589824 | tf_op jit(solution)/shard_map/all_to_all | solution.py:521
  (58 shorter events, 15.1 us)
Async XLA Ops:
  0.6 31.4 %copy-start.5 = (bf16[512,768]{1,0:T(8,128)(2,1)S(1)}, bf16[512,768]{1,0:T(8,128)(2,1)}, u32[]{:S(2)}) copy-start(bf16[512,768]{1,0:T(8,128)(2,1)} %sw_ref.1) | copy-start | bytes 2359300
  0.6 21.2 %collective-permute-start.3 = (bf16[144,1536]{1,0:T(8,128)(2,1)}, bf16[144,1536]{1,0:T(8,128)(2,1)S(1)}, u32[]{:S(2)}, u32[]{:S(2)}) collective-permute-start(bf16[144,1536]{1,0:T(8,128)(2,1)} %bitcast.11), channel_id=1, source_target_pairs={{0,64},{1,17},{16,80},{17,33},{32,96},{33,49},{48,112},{49,3},{2,6... | collective-permute-start | bytes 1327112 | tf_op jit(solution)/shard_map/ppermute | solution.py:30
  3.2 18.7 %collective-permute-start.4 = (bf16[144,1536]{1,0:T(8,128)(2,1)}, bf16[144,1536]{1,0:T(8,128)(2,1)S(1)}, u32[]{:S(2)}, u32[]{:S(2)}) collective-permute-start(bf16[144,1536]{1,0:T(8,128)(2,1)} %bitcast.12), channel_id=1, source_target_pairs={{0,128},{1,33},{16,144},{17,51},{32,160},{33,3},{48,176},{49,17},{... | collective-permute-start | bytes 1327112 | tf_op jit(solution)/shard_map/ppermute | solution.py:30
  6.2 15.7 %collective-permute-start.5 = (bf16[144,1536]{1,0:T(8,128)(2,1)}, bf16[144,1536]{1,0:T(8,128)(2,1)S(1)}, u32[]{:S(2)}, u32[]{:S(2)}) collective-permute-start(bf16[144,1536]{1,0:T(8,128)(2,1)} %bitcast.13), channel_id=1, source_target_pairs={{0,192},{1,51},{16,208},{17,1},{32,224},{33,17},{48,240},{49,33},{... | collective-permute-start | bytes 1327112 | tf_op jit(solution)/shard_map/ppermute | solution.py:30
  10.5 4.1 %collective-permute-start = (bf16[16,128]{1,0:T(8,128)(2,1)S(1)}, bf16[16,128]{1,0:T(8,128)(2,1)S(1)}, u32[]{:S(2)}, u32[]{:S(2)}) collective-permute-start(bf16[16,128]{1,0:T(8,128)(2,1)S(1)} %slice_select_fusion), channel_id=1, source_target_pairs={{0,12},{1,5},{16,28},{17,21},{32,44},{33,37},{48,60},{49,53},{2,14... | collective-permute-start | bytes 12296 | tf_op jit(solution)/shard_map/ppermute | solution.py:30
  14.6 7.1 %collective-permute-start.1 = (bf16[272,128]{1,0:T(8,128)(2,1)S(1)}, bf16[272,128]{1,0:T(8,128)(2,1)S(1)}, u32[]{:S(2)}, u32[]{:S(2)}) collective-permute-start(bf16[272,128]{1,0:T(8,128)(2,1)S(1)} %pad_maximum_fusion.ids_ref), channel_id=1, source_target_pairs={{0,2},{1,3},{16,18},{17,19},{32,34},{33,35},{48,50},{49,51},{2,0},... | collective-permute-start | bytes 208904 | tf_op jit(solution)/shard_map/ppermute | solution.py:30
  16.7 5.2 %collective-permute-start.2 = (bf16[272,128]{1,0:T(8,128)(2,1)S(1)}, bf16[272,128]{1,0:T(8,128)(2,1)S(1)}, u32[]{:S(2)}, u32[]{:S(2)}) collective-permute-start(bf16[272,128]{1,0:T(8,128)(2,1)S(1)} %pad_maximum_fusion.ids_ref), channel_id=1, source_target_pairs={{0,1},{1,0},{16,17},{17,16},{32,33},{33,32},{48,49},{49,48},{2,3},... | collective-permute-start | bytes 208904 | tf_op jit(solution)/shard_map/ppermute | solution.py:30
  21.9 3.7 %collective-permute-start.6 = (bf16[576,768]{1,0:T(8,128)(2,1)S(1)}, bf16[576,768]{1,0:T(8,128)(2,1)S(1)}, u32[]{:S(2)}, u32[]{:S(2)}) collective-permute-start(bf16[576,768]{1,0:T(8,128)(2,1)S(1)} %shard_map.95), channel_id=1, source_target_pairs={{0,1},{1,0},{16,17},{17,16},{32,33},{33,32},{48,49},{49,48},{2,3},... | collective-permute-start | bytes 2654216 | tf_op jit(solution)/shard_map/ppermute | solution.py:30
  25.7 19.0 %collective-permute-start.7 = (bf16[576,768]{1,0:T(8,128)(2,1)S(1)}, bf16[576,768]{1,0:T(8,128)(2,1)S(1)}, u32[]{:S(2)}, u32[]{:S(2)}) collective-permute-start(bf16[576,768]{1,0:T(8,128)(2,1)S(1)} %collective-permute-done.6.refs_0_.r), channel_id=1, source_target_pairs={{0,64},{1,17},{16,80},{17,33},{32,96},{33,49},{48,112},{49,3},{2,6... | collective-permute-start | bytes 2654216 | tf_op jit(solution)/shard_map/ppermute | solution.py:30
  28.6 16.1 %collective-permute-start.8 = (bf16[576,768]{1,0:T(8,128)(2,1)S(1)}, bf16[576,768]{1,0:T(8,128)(2,1)S(1)}, u32[]{:S(2)}, u32[]{:S(2)}) collective-permute-start(bf16[576,768]{1,0:T(8,128)(2,1)S(1)} %collective-permute-done.6.refs_0_.r), channel_id=1, source_target_pairs={{0,192},{1,51},{16,208},{17,1},{32,224},{33,17},{48,240},{49,33},{... | collective-permute-start | bytes 2654216 | tf_op jit(solution)/shard_map/ppermute | solution.py:30
  30.7 1.3 %collective-permute-start.10 = (bf16[272,128]{1,0:T(8,128)(2,1)S(1)}, bf16[272,128]{1,0:T(8,128)(2,1)S(1)}, u32[]{:S(2)}, u32[]{:S(2)}) collective-permute-start(bf16[272,128]{1,0:T(8,128)(2,1)S(1)} %collective-permute-done.1.far_ref), channel_id=1, source_target_pairs={{0,1},{1,0},{16,17},{17,16},{32,33},{33,32},{48,49},{49,48},{2,3},... | collective-permute-start | bytes 208904 | tf_op jit(solution)/shard_map/ppermute | solution.py:30
  30.7 5.0 %copy-start.3 = (bf16[3,48,1536]{2,1,0:T(8,128)(2,1)S(1)}, bf16[3,48,1536]{2,1,0:T(8,128)(2,1)}, u32[]{:S(2)}) copy-start(bf16[3,48,1536]{2,1,0:T(8,128)(2,1)} %param.10) | copy-start | bytes 1327108
  30.8 13.9 %collective-permute-start.9 = (bf16[144,768]{1,0:T(8,128)(2,1)S(1)}, bf16[144,768]{1,0:T(8,128)(2,1)S(1)}, u32[]{:S(2)}, u32[]{:S(2)}) collective-permute-start(bf16[144,768]{1,0:T(8,128)(2,1)S(1)} %shard_map.96), channel_id=1, source_target_pairs={{0,128},{1,33},{16,144},{17,51},{32,160},{33,3},{48,176},{49,17},{... | collective-permute-start | bytes 663560 | tf_op jit(solution)/shard_map/ppermute | solution.py:30
  44.7 2.1 %collective-permute-start.11 = (bf16[288,768]{1,0:T(8,128)(2,1)S(1)}, bf16[288,768]{1,0:T(8,128)(2,1)S(1)}, u32[]{:S(2)}, u32[]{:S(2)}) collective-permute-start(bf16[288,768]{1,0:T(8,128)(2,1)S(1)} %shard_map.99), channel_id=1, source_target_pairs={{0,1},{1,0},{16,17},{17,16},{32,33},{33,32},{48,49},{49,48},{2,3},... | collective-permute-start | bytes 1327112 | tf_op jit(solution)/shard_map/ppermute | solution.py:30
  48.4 2.4 %copy-start.1 = (bf16[1536,512]{1,0:T(8,128)(2,1)S(1)}, bf16[1536,512]{1,0:T(8,128)(2,1)}, u32[]{:S(2)}) copy-start(bf16[1536,512]{1,0:T(8,128)(2,1)} %wq.1) | copy-start | bytes 4718596
  48.5 2.4 %copy-start.2 = (bf16[1536,192]{0,1:T(8,128)(2,1)S(1)}, bf16[1536,192]{0,1:T(8,128)(2,1)}, u32[]{:S(2)}) copy-start(bf16[1536,192]{0,1:T(8,128)(2,1)} %param.13) | copy-start | bytes 1769476
  48.5 2.4 %collective-permute-start.12 = (bf16[512,768]{1,0:T(8,128)(2,1)S(1)}, bf16[512,768]{1,0:T(8,128)(2,1)S(1)}, u32[]{:S(2)}, u32[]{:S(2)}) collective-permute-start(bf16[512,768]{1,0:T(8,128)(2,1)S(1)} %shard_map.101), channel_id=1, source_target_pairs={{0,1},{1,0},{16,17},{17,16},{32,33},{33,32},{48,49},{49,48},{2,3},... | collective-permute-start | bytes 2359304 | tf_op jit(solution)/shard_map/ppermute | solution.py:30
  50.4 5.5 %copy-start.6 = (bf16[1,256,1536]{2,1,0:T(8,128)(2,1)S(1)}, bf16[1,256,1536]{2,1,0:T(8,128)(2,1)}, u32[]{:S(2)}) copy-start(bf16[1,256,1536]{2,1,0:T(8,128)(2,1)} %param.15) | copy-start | bytes 2359300
  52.6 3.9 %collective-permute-start.13 = (bf16[1792,128]{1,0:T(8,128)(2,1)S(1)}, bf16[1792,128]{1,0:T(8,128)(2,1)S(1)}, u32[]{:S(2)}, u32[]{:S(2)}) collective-permute-start(bf16[1792,128]{1,0:T(8,128)(2,1)S(1)} %get-tuple-element.67), channel_id=1, source_target_pairs={{0,1},{1,0},{16,17},{17,16},{32,33},{33,32},{48,49},{49,48},{2,3},... | collective-permute-start | bytes 1376264 | tf_op jit(solution)/shard_map/ppermute | solution.py:30
  52.8 9.7 %collective-permute-start.14 = (bf16[1280,128]{1,0:T(8,128)(2,1)S(1)}, bf16[1280,128]{1,0:T(8,128)(2,1)S(1)}, u32[]{:S(2)}, u32[]{:S(2)}) collective-permute-start(bf16[1280,128]{1,0:T(8,128)(2,1)S(1)} %get-tuple-element.68.refs_2_), channel_id=1, source_target_pairs={{0,4},{1,13},{16,20},{17,29},{32,36},{33,45},{48,52},{49,61},{2,6}... | collective-permute-start | bytes 983048 | tf_op jit(solution)/shard_map/ppermute | solution.py:30
  55.9 8.5 %collective-permute-start.15 = (bf16[1280,128]{1,0:T(8,128)(2,1)S(1)}, bf16[1280,128]{1,0:T(8,128)(2,1)S(1)}, u32[]{:S(2)}, u32[]{:S(2)}) collective-permute-start(bf16[1280,128]{1,0:T(8,128)(2,1)S(1)} %get-tuple-element.68.refs_2_), channel_id=1, source_target_pairs={{0,12},{1,5},{16,28},{17,21},{32,44},{33,37},{48,60},{49,53},{2,14... | collective-permute-start | bytes 983048 | tf_op jit(solution)/shard_map/ppermute | solution.py:30
  55.9 20.6 %collective-permute-start.20 = (bf16[256,1536]{1,0:T(8,128)(2,1)S(1)}, bf16[256,1536]{1,0:T(8,128)(2,1)S(1)}, u32[]{:S(2)}, u32[]{:S(2)}) collective-permute-start(bf16[256,1536]{1,0:T(8,128)(2,1)S(1)} %bitcast.15), channel_id=1, source_target_pairs={{0,1},{1,0},{16,17},{17,16},{32,33},{33,32},{48,49},{49,48},{2,3},... | collective-permute-start | bytes 2359304 | tf_op jit(solution)/shard_map/ppermute | solution.py:30
  64.4 4.7 %collective-permute-start.17 = (bf16[1280,128]{1,0:T(8,128)(2,1)S(1)}, bf16[1280,128]{1,0:T(8,128)(2,1)S(1)}, u32[]{:S(2)}, u32[]{:S(2)}) collective-permute-start(bf16[1280,128]{1,0:T(8,128)(2,1)S(1)} %collective-permute-done.14.refs_2_), channel_id=1, source_target_pairs={{0,1},{1,0},{16,17},{17,16},{32,33},{33,32},{48,49},{49,48},{2,3},... | collective-permute-start | bytes 983048 | tf_op jit(solution)/shard_map/ppermute | solution.py:30
  64.4 4.7 %collective-permute-start.18 = (bf16[1280,128]{1,0:T(8,128)(2,1)S(1)}, bf16[1280,128]{1,0:T(8,128)(2,1)S(1)}, u32[]{:S(2)}, u32[]{:S(2)}) collective-permute-start(bf16[1280,128]{1,0:T(8,128)(2,1)S(1)} %collective-permute-done.15.refs_3_), channel_id=1, source_target_pairs={{0,1},{1,0},{16,17},{17,16},{32,33},{33,32},{48,49},{49,48},{2,3},... | collective-permute-start | bytes 983048 | tf_op jit(solution)/shard_map/ppermute | solution.py:30
  64.9 6.3 %collective-permute-start.16 = (bf16[1280,128]{1,0:T(8,128)(2,1)S(1)}, bf16[1280,128]{1,0:T(8,128)(2,1)S(1)}, u32[]{:S(2)}, u32[]{:S(2)}) collective-permute-start(bf16[1280,128]{1,0:T(8,128)(2,1)S(1)} %collective-permute-done.14.refs_2_), channel_id=1, source_target_pairs={{0,4},{1,13},{16,20},{17,29},{32,36},{33,45},{48,52},{49,61},{2,6}... | collective-permute-start | bytes 983048 | tf_op jit(solution)/shard_map/ppermute | solution.py:30
  71.2 11.9 %copy-start = (bf16[1536,768]{1,0:T(8,128)(2,1)S(1)}, bf16[1536,768]{1,0:T(8,128)(2,1)}, u32[]{:S(2)}) copy-start(bf16[1536,768]{1,0:T(8,128)(2,1)} %w.1) | copy-start | bytes 7077892
  71.2 3.2 %collective-permute-start.19 = (bf16[1280,128]{1,0:T(8,128)(2,1)S(1)}, bf16[1280,128]{1,0:T(8,128)(2,1)S(1)}, u32[]{:S(2)}, u32[]{:S(2)}) collective-permute-start(bf16[1280,128]{1,0:T(8,128)(2,1)S(1)} %collective-permute-done.16.refs_2_), channel_id=1, source_target_pairs={{0,1},{1,0},{16,17},{17,16},{32,33},{33,32},{48,49},{49,48},{2,3},... | collective-permute-start | bytes 983048 | tf_op jit(solution)/shard_map/ppermute | solution.py:30
  78.2 7.5 %collective-permute-start.22 = (bf16[384,384]{1,0:T(8,128)(2,1)S(1)}, bf16[384,384]{1,0:T(8,128)(2,1)S(1)}, u32[]{:S(2)}, u32[]{:S(2)}) collective-permute-start(bf16[384,384]{1,0:T(8,128)(2,1)S(1)} %get-tuple-element.85), channel_id=1, source_target_pairs={{0,128},{1,9},{16,144},{17,25},{32,160},{33,41},{48,176},{49,57},{... | collective-permute-start | bytes 884744 | tf_op jit(solution)/shard_map/ppermute | solution.py:30
  78.8 10.0 %collective-permute-start.23 = (bf16[384,384]{1,0:T(8,128)(2,1)S(1)}, bf16[384,384]{1,0:T(8,128)(2,1)S(1)}, u32[]{:S(2)}, u32[]{:S(2)}) collective-permute-start(bf16[384,384]{1,0:T(8,128)(2,1)S(1)} %get-tuple-element.83), channel_id=1, source_target_pairs={{0,64},{1,5},{16,80},{17,21},{32,96},{33,37},{48,112},{49,53},{2,6... | collective-permute-start | bytes 884744 | tf_op jit(solution)/shard_map/ppermute | solution.py:30
  80.4 8.4 %collective-permute-start.24 = (bf16[384,384]{1,0:T(8,128)(2,1)S(1)}, bf16[384,384]{1,0:T(8,128)(2,1)S(1)}, u32[]{:S(2)}, u32[]{:S(2)}) collective-permute-start(bf16[384,384]{1,0:T(8,128)(2,1)S(1)} %get-tuple-element.86), channel_id=1, source_target_pairs={{0,192},{1,13},{16,208},{17,29},{32,224},{33,45},{48,240},{49,61},... | collective-permute-start | bytes 884744 | tf_op jit(solution)/shard_map/ppermute | solution.py:30
  81.5 1.6 %collective-permute-start.21 = (bf16[256,384]{1,0:T(8,128)(2,1)S(1)}, bf16[256,384]{1,0:T(8,128)(2,1)S(1)}, u32[]{:S(2)}, u32[]{:S(2)}) collective-permute-start(bf16[256,384]{1,0:T(8,128)(2,1)S(1)} %slice.11), channel_id=1, source_target_pairs={{0,1},{1,0},{16,17},{17,16},{32,33},{33,32},{48,49},{49,48},{2,3},... | collective-permute-start | bytes 589832 | tf_op jit(solution)/shard_map/ppermute | solution.py:30
  110.6 2.0 %collective-permute-start.25 = (f32[6,384]{1,0:T(8,128)S(1)}, f32[6,384]{1,0:T(8,128)S(1)}, u32[]{:S(2)}, u32[]{:S(2)}) collective-permute-start(f32[6,384]{1,0:T(8,128)S(1)} %get-tuple-element.93), channel_id=1, source_target_pairs={{0,1},{1,0},{16,17},{17,16},{32,33},{33,32},{48,49},{49,48},{2,3},... | collective-permute-start | bytes 27656 | tf_op jit(solution)/shard_map/ppermute | solution.py:30
  (1 other events, 2.4 us)
